TPU v7x, 32 devices: a whole 2x2x4 slice. The times are simulated.
32 devices in a mesh: groups: 2 (over x), tp: 4 (over y, core), dp: 4 (over z).
Axes of the slice: x: 2, y: 2, z: 4, core: 2. Of those that a mesh axis runs over, the one named last changes fastest.
Arguments:
- filter_feed_series: bfloat16 [4, 64, 8192], P(None, ('groups', 'dp'), 'tp'), parts along dimension 1, may hold values from -6 to 6
- valve_branch_series: bfloat16 [4, 64, 8192], P(None, ('groups', 'dp'), 'tp'), parts along dimension 1, may hold values from -6 to 6
- raw_increment_entries: bfloat16 [4, 64, 8192], P(None, ('groups', 'dp'), 'tp'), parts along dimension 1, may hold values from -6 to 6
- entering_memory_matrix: float32 [4, 64, 16], P(None, ('groups', 'dp')), parts along dimension 1, may hold values from -6 to 6
- leaving_memory_matrix: float32 [4, 64, 16], P(None, ('groups', 'dp')), parts along dimension 1, may hold values from -6 to 6
- emission_matrix: bfloat16 [8192, 4096], P('tp'), may hold values from -0.0625 to 0.0625
- recurrent_memory: float32 [8192, 1024], P('tp', ('groups', 'dp')), parts along dimension 1, may hold values from -6 to 6
- filter_recent_history: float32 [8192, 256], P('tp', ('groups', 'dp')), parts along dimension 1, may hold values from -6 to 6
- logarithmic_fading_speeds: float32 [8192, 16], replicated, may hold values from -2 to 2.7
- filter_coefficients: float32 [8192, 4], replicated, may hold values from -3 to 3
- filter_offset_term: float32 [8192], replicated, may hold values from -1 to 1
- increment_offset_term: float32 [8192], replicated, may hold values from -3 to 0.5
- residual_factor: float32 [8192], replicated, may hold values from 0.5 to 1.5
- remaining_ranks: int32 [3], replicated, may hold values from 0 to 3, as said below
- holder_segment_tallies: int32 [3], replicated, may hold values from 1 to 23, 64 in all
Outputs:
- decoded: bfloat16 [4, 64, 4096], P(None, ('groups', 'dp')), parts along dimension 1
- relocated_emission_matrix: bfloat16 [23552, 4096], P(('groups', 'tp')), parts along dimension 0
- relocated_recurrent_memory: float32 [11776, 1024], P('tp', ('groups', 'dp')), parts along dimension 1
- relocated_filter_history: float32 [11776, 256], P('tp', ('groups', 'dp')), parts along dimension 1
There are 2 independent parts, one for each index of `groups`. A program takes and returns all parts, laid end to end along the dimension named above; an argument that names none is the same for every part. Nothing has to cross between parts.
Inputs may be any that keep to these rules, and one draw needn't show every extreme that they name: `remaining_ranks`: 3 distinct tp indices in increasing order; the first and the last index of tp are always among them. `holder_segment_tallies`: sums to 64; some owner has exactly 23 blocks.
All inputs are finite; a program needn't handle non-finite values.
Results may differ from a plain program's by a relative error of at most 0.008.
Values may be sent and summed in bfloat16 or wider, within the bound.
No kernel may reach another device: no remote copies, remote signals or barrier semaphores. Data moves between devices by JAX's collectives and lax.ppermute only.
A program may use at most 192 MiB of HBM per device.

v0:
```python
import jax
import jax.numpy as jnp
from jax import lax
from jax.experimental import pallas as pl
from jax.experimental.pallas import tpu as pltpu
from jax.sharding import PartitionSpec as P

BLOCK = 128
UNIT = 16
BF = jnp.bfloat16
F32 = jnp.float32
AXES = ("groups", "tp", "dp")


def owner_ranges(remaining_ranks, holder_segment_tallies, holder_ranks):
    starts = jnp.cumsum(holder_segment_tallies) - holder_segment_tallies
    roster = jnp.arange(holder_ranks, dtype=jnp.int32)
    match = (remaining_ranks[None, :] == roster[:, None]).astype(jnp.int32)
    first = jnp.sum(match * starts[None, :], axis=1)
    total = jnp.sum(match * holder_segment_tallies[None, :], axis=1)
    return first, total


def pack_rows(columns, first, total, slot_rows):
    padded = jnp.pad(columns, ((0, slot_rows), (0, 0)))
    places = jnp.arange(slot_rows, dtype=jnp.int32)

    def one_owner(start, count):
        rows = lax.dynamic_slice_in_dim(padded, start * BLOCK, slot_rows, 0)
        return jnp.where((places < count * BLOCK)[:, None], rows, jnp.zeros_like(rows))

    packed = jax.vmap(one_owner)(first, total)
    return packed.reshape(-1, columns.shape[1])


def relocate_everywhere(rows, first, total, slot_rows):
    spread = lax.all_to_all(rows, "tp", split_axis=1, concat_axis=0, tiled=True)
    packed = pack_rows(spread, first, total, slot_rows)
    return lax.all_to_all(packed, "tp", split_axis=0, concat_axis=1, tiled=True)


def decode_plain(x, z, dt, enter, leave, ssm, conv, logs, taps, offs, inc, res, weights):
    steps, seqs, channels = x.shape
    h = ssm.reshape(channels, seqs, -1)
    window = conv.reshape(channels, seqs, 4)
    decay = -jnp.exp(logs)
    gated = []
    for step in range(steps):
        now = x[step].astype(F32).T
        window = jnp.concatenate([window[:, :, 1:], now[:, :, None]], axis=2)
        inner = jax.nn.silu(jnp.sum(window * taps[:, None, :], axis=2) + offs[:, None])
        delta = jax.nn.softplus(dt[step].astype(F32).T + inc[:, None])
        h = (
            jnp.exp(delta[:, :, None] * decay[:, None, :]) * h
            + (delta * inner)[:, :, None] * enter[step][None, :, :]
        )
        y = jnp.sum(h * leave[step][None, :, :], axis=2) + res[:, None] * inner
        gated.append((y * jax.nn.silu(z[step].astype(F32).T)).astype(BF))
    gated = jnp.concatenate(gated, axis=1)
    partial = lax.dot_general(
        gated, weights, (((0,), (0,)), ((), ())), preferred_element_type=F32
    )
    return partial, h.reshape(channels, -1), window.reshape(channels, -1)


def general(x, z, dt, enter, leave, w, ssm, conv, logs, taps, offs, inc, res, ranks, tallies):
    holders = lax.axis_size("tp")
    mine = lax.axis_index("tp")
    width, old = logs.shape[0], w.shape[0]
    slot_rows = (width // BLOCK // (holders * 3 // 4) + 2) * BLOCK
    first, total = owner_ranges(ranks, tallies, holders)

    def own(a):
        return lax.dynamic_slice_in_dim(a, mine * old, old, 0)

    moved_w = relocate_everywhere(w, first, total, slot_rows)
    partial, ssm, conv = decode_plain(
        x, z, dt, enter, leave, ssm, conv, own(logs), own(taps), own(offs), own(inc), own(res), w
    )
    decoded = lax.psum(partial, "tp").astype(BF).reshape(x.shape[0], x.shape[1], -1)
    return (
        decoded,
        moved_w,
        relocate_everywhere(ssm, first, total, slot_rows),
        relocate_everywhere(conv, first, total, slot_rows),
    )


def each(low, high, act):
    lax.fori_loop(low, high, lambda b, _: (act(b), 0)[1], 0)


CHUNK = 256
WIDE = 2048


def decode_kernel(
    sc, x, z, dt, enter, leave, h0, hist, logs, taps, offs, inc, res, w_all,
    out_w, side, second, third, partial, states, ys, deltas, feeds, turned, w, w_sem, own_sem, side_sem, cut_sem,
):
    i = pl.program_id(0)
    steps, seqs, chunk = x.shape
    latents = logs.shape[0]
    per = chunk // BLOCK
    blocks = w_all.shape[0] // BLOCK
    slots = out_w.shape[0] // BLOCK
    side_n = side.shape[0] // BLOCK
    own_src, own_n, own_dst, side_src = sc[1], sc[2], sc[3], sc[11]

    def rows(b):
        return pl.ds(pl.multiple_of(b * BLOCK, BLOCK), BLOCK)

    def fetch(b):
        return pltpu.make_async_copy(w_all.at[rows(b)], w.at[rows(b)], w_sem.at[b])

    def keep(b):
        at = jnp.clip(b - own_src + own_dst, 0, slots - 1)
        return pltpu.make_async_copy(w.at[rows(b)], out_w.at[rows(at)], own_sem.at[b])

    def pass_on(b):
        at = jnp.clip(b - side_src, 0, side_n - 1)
        return pltpu.make_async_copy(w.at[rows(b)], side.at[rows(at)], side_sem.at[b])

    @pl.when(i == 0)
    def _():
        each(0, blocks, lambda b: fetch(b).start())
        partial[...] = jnp.zeros_like(partial)

    decay = -jnp.exp(logs[...])
    xs = [x[t].astype(F32) for t in range(steps)]
    window = [hist[k] for k in range(1, 4)] + xs
    tap = [taps[k : k + 1, :] for k in range(4)]
    inners = []
    for t in range(steps):
        mixed = offs[...] + sum(window[t + k] * tap[k] for k in range(4))
        inner = mixed / (1.0 + jnp.exp(-mixed))
        v = dt[t].astype(F32) + inc[...]
        delta = jnp.maximum(v, 0.0) + jnp.log1p(jnp.exp(-jnp.abs(v)))
        inners.append(inner)
        deltas[t * seqs : (t + 1) * seqs, :] = delta
        feeds[t * seqs : (t + 1) * seqs, :] = delta * inner
    turned[...] = h0[...].T

    def wide(a):
        return jnp.concatenate([a] * per, axis=1)

    def sequence(s, _):
        at = pl.ds(pl.multiple_of(s * latents, latents), latents)
        h = turned[at, :]
        for t in range(steps):
            c = t * seqs + s
            row = pl.ds(c, 1)
            h = jnp.exp(deltas[row, :] * decay) * h + feeds[row, :] * wide(enter[c])
            ys[row, :] = jnp.sum(h * wide(leave[c]), axis=0, keepdims=True)
        states[at, :] = h.astype(BF)
        return 0

    lax.fori_loop(0, seqs, sequence, 0)
    states[seqs * latents :, :] = jnp.concatenate(xs, axis=0).astype(BF)
    gated = []
    for t in range(steps):
        y = ys[t * seqs : (t + 1) * seqs, :] + res[...] * inners[t]
        g = z[t].astype(F32)
        gated.append(y * (g / (1.0 + jnp.exp(-g))))
    gated = jnp.concatenate(gated, axis=0).astype(BF)

    def arrived(j, _):
        b = i * per + j
        fetch(b).wait()

        @pl.when((b >= own_src) & (b < own_src + own_n))
        def _():
            keep(b).start()

        @pl.when((b >= side_src) & (b < side_src + side_n))
        def _():
            pass_on(b).start()

        return 0

    lax.fori_loop(0, per, arrived, 0)
    last = i == pl.num_programs(0) - 1
    cuts = [
        pltpu.make_async_copy(
            w.at[pl.ds(pl.multiple_of(sc[row], UNIT), to.shape[0])], to, cut_sem.at[k]
        )
        for k, (row, to) in enumerate(((13, second), (14, third)))
    ]

    @pl.when(last)
    def _():
        for copy in cuts:
            copy.start()

    here = pl.ds(pl.multiple_of(i * chunk, chunk), chunk)

    def project(k):
        cols = pl.ds(pl.multiple_of(k * WIDE, WIDE), WIDE)
        partial[:, cols] += jnp.dot(gated, w[here, cols], preferred_element_type=F32)

    each(0, partial.shape[1] // WIDE, project)

    @pl.when(last)
    def _():
        for copy in cuts:
            copy.wait()
        each(own_src, own_src + own_n, lambda b: keep(b).wait())
        each(side_src, jnp.minimum(side_src + side_n, blocks), lambda b: pass_on(b).wait())


def decode_here(scalars, slots, side_n, cut_rows, x, z, dt, enter, leave, w, ssm, conv, logs, taps, offs, inc, res):
    steps, seqs, channels = x.shape
    latents = logs.shape[1]
    features = w.shape[1]
    n = channels // CHUNK
    series = pl.BlockSpec((steps, seqs, CHUNK), lambda i, sc: (0, 0, i))
    small = pl.BlockSpec((steps * seqs, latents, BLOCK), lambda i, sc: (0, 0, 0))

    def lanes(rows):
        return pl.BlockSpec((rows, CHUNK), lambda i, sc: (0, sc[0] * n + i))

    grid_spec = pltpu.PrefetchScalarGridSpec(
        num_scalar_prefetch=1,
        grid=(n,),
        in_specs=[
            series, series, series, small, small,
            pl.BlockSpec((CHUNK, seqs * latents), lambda i, sc: (i, 0)),
            pl.BlockSpec((4, seqs, CHUNK), lambda i, sc: (0, 0, i)),
            lanes(latents), lanes(4), lanes(1), lanes(1), lanes(1),
            pl.BlockSpec(memory_space=pltpu.HBM),
        ],
        out_specs=[
            pl.BlockSpec(memory_space=pltpu.HBM),
            pl.BlockSpec(memory_space=pltpu.HBM),
            pl.BlockSpec(memory_space=pltpu.HBM),
            pl.BlockSpec(memory_space=pltpu.HBM),
            pl.BlockSpec((steps * seqs, features), lambda i, sc: (0, 0)),
            pl.BlockSpec((seqs * (latents + 4), CHUNK), lambda i, sc: (0, i)),
        ],
        scratch_shapes=[
            pltpu.VMEM((steps * seqs, CHUNK), F32),
            pltpu.VMEM((steps * seqs, CHUNK), F32),
            pltpu.VMEM((steps * seqs, CHUNK), F32),
            pltpu.VMEM((seqs * latents, CHUNK), F32),
            pltpu.VMEM((channels, features), BF),
            pltpu.SemaphoreType.DMA((channels // BLOCK,)),
            pltpu.SemaphoreType.DMA((channels // BLOCK,)),
            pltpu.SemaphoreType.DMA((channels // BLOCK,)),
            pltpu.SemaphoreType.DMA((2,)),
        ],
    )
    rows = steps * seqs
    return pl.pallas_call(
        decode_kernel,
        grid_spec=grid_spec,
        out_shape=(
            jax.ShapeDtypeStruct((slots * BLOCK, features), BF),
            jax.ShapeDtypeStruct((side_n * BLOCK, features), BF),
            jax.ShapeDtypeStruct((cut_rows[0], features), BF),
            jax.ShapeDtypeStruct((cut_rows[1], features), BF),
            jax.ShapeDtypeStruct((rows, features), F32),
            jax.ShapeDtypeStruct((seqs * (latents + 4), channels), BF),
        ),
        compiler_params=pltpu.CompilerParams(vmem_limit_bytes=50 << 20),
        cost_estimate=HINT,
        name="decode",
    )(
        scalars, x, z, dt,
        jnp.broadcast_to(enter.reshape(rows, latents, 1), (rows, latents, BLOCK)),
        jnp.broadcast_to(leave.reshape(rows, latents, 1), (rows, latents, BLOCK)),
        ssm, conv.T.reshape(seqs, 4, channels).transpose(1, 0, 2), logs.T, taps.T,
        offs.reshape(1, -1), inc.reshape(1, -1), res.reshape(1, -1), w,
    )


HINT = pl.CostEstimate(flops=0, bytes_accessed=1024, transcendentals=0)


def cut_rows(scalars, w, rows):
    def kernel(sc, w_ref, out, sem):
        copy = pltpu.make_async_copy(
            w_ref.at[pl.ds(pl.multiple_of(sc[12], UNIT), rows)], out, sem
        )
        copy.start()
        copy.wait()

    return pl.pallas_call(
        kernel,
        grid_spec=pltpu.PrefetchScalarGridSpec(
            num_scalar_prefetch=1,
            grid=(),
            in_specs=[pl.BlockSpec(memory_space=pltpu.HBM)],
            out_specs=pl.BlockSpec(memory_space=pltpu.VMEM),
            scratch_shapes=[pltpu.SemaphoreType.DMA],
        ),
        out_shape=jax.ShapeDtypeStruct((rows, w.shape[1]), w.dtype),
        compiler_params=pltpu.CompilerParams(vmem_limit_bytes=8 << 20),
        cost_estimate=HINT,
        name="cut_rows",
    )(scalars, w)


def place_rows(scalars, out_w, pieces, side=None, blanks=False):
    slots, features = out_w.shape[0] // BLOCK, out_w.shape[1]
    arrays = []
    for piece in pieces:
        if not any(piece[0] is a for a in arrays):
            arrays.append(piece[0])
    jobs = []
    for array, first, rows, offset in pieces:
        jobs.append((next(k for k, a in enumerate(arrays) if a is array), first, rows, offset))
    side_n = 0 if side is None else side.shape[0] // BLOCK
    operands = arrays + ([] if side is None else [side])
    staged = sum(job[2] for job in jobs)

    def kernel(sc, *refs):
        ins, out = refs[: len(operands)], refs[len(operands) + 1]
        stage, side_stage, sems, side_sems, blank, blank_sems = refs[len(operands) + 2 :]
        recv, row0, q = sc[5], sc[6], sc[7]
        c_src, c_n, c_dst = sc[8], sc[9], sc[10]
        starts = [sum(job[2] for job in jobs[:k]) for k in range(len(jobs))]

        def fetch(k):
            which, first, rows, _ = jobs[k]
            return pltpu.make_async_copy(
                ins[which].at[pl.ds(first, rows)],
                stage.at[pl.ds(starts[k], rows)],
                sems.at[2 * k],
            )

        def store(k):
            _, _, rows, offset = jobs[k]
            row = jnp.clip(row0 + offset(q) * UNIT, 0, slots * BLOCK - rows)
            return pltpu.make_async_copy(
                stage.at[pl.ds(starts[k], rows)],
                out.at[pl.ds(pl.multiple_of(row, UNIT), rows)],
                sems.at[2 * k + 1],
            )

        def side_fetch(b):
            src = jnp.clip(c_src + b, 0, side_n - 1) * BLOCK
            return pltpu.make_async_copy(
                ins[-1].at[pl.ds(pl.multiple_of(src, BLOCK), BLOCK)],
                side_stage.at[pl.ds(pl.multiple_of(b * BLOCK, BLOCK), BLOCK)],
                side_sems.at[2 * b],
            )

        def side_store(b):
            dst = jnp.clip(c_dst + b, 0, slots - 1) * BLOCK
            return pltpu.make_async_copy(
                side_stage.at[pl.ds(pl.multiple_of(b * BLOCK, BLOCK), BLOCK)],
                out.at[pl.ds(pl.multiple_of(dst, BLOCK), BLOCK)],
                side_sems.at[2 * b + 1],
            )

        def clear(b):
            return pltpu.make_async_copy(
                blank, out.at[pl.ds(pl.multiple_of(b * BLOCK, BLOCK), BLOCK)], blank_sems.at[b]
            )

        if blanks:
            blank[...] = jnp.zeros_like(blank)
            each(sc[4], slots, lambda b: clear(b).start())

        @pl.when(recv == 1)
        def _():
            for k in range(len(jobs)):
                fetch(k).start()
            for k in range(len(jobs)):
                fetch(k).wait()
                store(k).start()
            for k in range(len(jobs)):
                store(k).wait()

        if side_n:
            count = jnp.minimum(c_n, side_n)
            each(0, count, lambda b: side_fetch(b).start())

            def pass_on(b):
                side_fetch(b).wait()
                side_store(b).start()

            each(0, count, pass_on)
            each(0, count, lambda b: side_store(b).wait())

        if blanks:
            each(sc[4], slots, lambda b: clear(b).wait())

    any_spec = pl.BlockSpec(memory_space=pl.ANY)
    side_rows = max(side_n * BLOCK, UNIT)
    return pl.pallas_call(
        kernel,
        grid_spec=pltpu.PrefetchScalarGridSpec(
            num_scalar_prefetch=1,
            grid=(),
            in_specs=[any_spec] * (len(operands) + 1),
            out_specs=any_spec,
            scratch_shapes=[
                pltpu.VMEM((staged, features), out_w.dtype),
                pltpu.VMEM((side_rows, features), out_w.dtype),
                pltpu.SemaphoreType.DMA((2 * len(jobs),)),
                pltpu.SemaphoreType.DMA((2 * max(side_n, 1),)),
                pltpu.VMEM((BLOCK if blanks else UNIT, features), out_w.dtype),
                pltpu.SemaphoreType.DMA((slots,)),
            ],
        ),
        out_shape=jax.ShapeDtypeStruct(out_w.shape, out_w.dtype),
        input_output_aliases={len(operands) + 1: 0},
        compiler_params=pltpu.CompilerParams(
            vmem_limit_bytes=(staged + side_rows + BLOCK) * features * 2 + (2 << 20)
        ),
        cost_estimate=HINT,
        name="place_rows",
    )(scalars, *operands, out_w)


def place_states(scalars, slots, own, side, across, latent_rows):
    rows = own.shape[0]
    seqs = (rows - latent_rows) // 4

    def kernel(sc, own_ref, side_ref, across_ref, ssm, conv, turned):
        own_src, own_n, own_dst, filled = sc[1], sc[2], sc[3], sc[4]
        recv, recv_dst = sc[5], sc[6] // BLOCK
        c_src, c_n, c_dst = sc[8], sc[9], sc[10]

        def rows_of(b):
            return pl.ds(pl.multiple_of(b * BLOCK, BLOCK), BLOCK)

        def put(b, ref, at):
            block = ref[:, rows_of(at)].astype(F32)
            ssm[rows_of(b), :] = block[:latent_rows].T
            for k in range(4):
                at = latent_rows + k * seqs
                turned[pl.ds(k, seqs, stride=4), :] = block[at : at + seqs]
            conv[:, rows_of(b)] = turned[...]

        across_n = across_ref.shape[1] // BLOCK

        def empty(b):
            ssm[rows_of(b), :] = jnp.zeros((BLOCK, latent_rows), F32)
            conv[:, rows_of(b)] = jnp.zeros((rows - latent_rows, BLOCK), F32)

        first = jnp.where(recv == 1, recv_dst, 0)
        count = jnp.where(recv == 1, across_n, 0)
        each(own_dst, own_dst + own_n, lambda b: put(b, own_ref, b - own_dst + own_src))
        each(c_dst, c_dst + c_n, lambda b: put(b, side_ref, b - c_dst + c_src))
        each(first, first + count, lambda b: put(b, across_ref, b - recv_dst))
        each(filled, slots, empty)

    vmem = pl.BlockSpec(memory_space=pltpu.VMEM)
    return pl.pallas_call(
        kernel,
        grid_spec=pltpu.PrefetchScalarGridSpec(
            num_scalar_prefetch=1,
            grid=(),
            in_specs=[vmem] * 3,
            out_specs=[vmem] * 2,
            scratch_shapes=[pltpu.VMEM((rows - latent_rows, BLOCK), F32)],
        ),
        out_shape=(
            jax.ShapeDtypeStruct((slots * BLOCK, latent_rows), F32),
            jax.ShapeDtypeStruct((rows - latent_rows, slots * BLOCK), F32),
        ),
        compiler_params=pltpu.CompilerParams(vmem_limit_bytes=24 << 20),
        cost_estimate=HINT,
        name="place_states",
    )(scalars, own, side, across)


def split(blocks):
    return blocks, (5 * blocks + 5) // 11


def neighbours(x, z, dt, enter, leave, w, ssm, conv, logs, taps, offs, inc, res, ranks, tallies):
    groups, depth = lax.axis_size("groups"), lax.axis_size("dp")
    old_blocks = w.shape[0] // BLOCK
    cap = (logs.shape[0] // BLOCK) // 3 + 2
    most = cap - old_blocks
    half = 2 * old_blocks
    fewest = half - cap

    def place(a, b, c):
        return (a * 4 + b) * depth + c

    every = [(a, c) for a in range(groups) for c in range(depth)]
    across = [(place(a, u, c), place(a, 3 - u, c)) for a, c in every for u in (1, 2)]
    along_x = [(place(a, u, c), place(1 - a, u, c)) for a, c in every for u in (1, 2)]
    along_z = [(place(a, u, c), place(a, u, c ^ 1)) for a, c in every for u in (1, 2)]
    inside = [(place(a, u, c), place(a, v, c)) for a, c in every for u, v in ((1, 0), (2, 3))]
    cores = [(place(a, u, c), place(a, u ^ 1, c)) for a, c in every for u in range(4)]
    chips = [(place(a, u, c), place(a, u ^ 2, c)) for a, c in every for u in range(4)]

    def plan(ranks, tallies, pick, scalars, lane0, lane1):
        g, t, d = (lax.axis_index(a) for a in AXES)
        q = 2 * g + (d & 1)
        middle, t0, t1, t2 = ranks[1], tallies[0], tallies[1], tallies[2]
        is_mid = (t == middle).astype(jnp.int32)
        crossing = jnp.where(middle == 2, half - t0, half - t2)
        def by_rank(first, low, high, last):
            return jnp.where(t == 0, first, jnp.where(t == 3, last, jnp.where(t == 1, low, high)))

        pick[0] = jnp.clip(crossing - fewest, 0, old_blocks - 2 - fewest)
        base = jnp.where(t == 1, (old_blocks - crossing) * BLOCK, 0)
        early, relay = split(crossing)
        lane0[0] = base
        lane1[0] = by_rank(0, 0, (old_blocks - most) * BLOCK, 0)

        values = [
            t,
            0,
            by_rank(old_blocks, is_mid * (half - t0), is_mid * (half - t2), old_blocks),
            by_rank(0, 0, crossing, t2 - old_blocks),
            by_rank(t0, is_mid * t1, is_mid * t1, t2),
            is_mid,
            by_rank(0, (half - t0) * BLOCK, 0, 0),
            q,
            by_rank(0, 0, 0, most - (t2 - old_blocks)),
            by_rank(t0 - old_blocks, 0, 0, t2 - old_blocks),
            by_rank(old_blocks, 0, 0, 0),
            by_rank(2 * old_blocks, 0, old_blocks - most, 2 * old_blocks),
            base + 2 * crossing * q * UNIT,
            base + (2 * crossing * q + early) * UNIT,
            base + (2 * crossing * (3 - q) + 2 * relay) * UNIT,
        ]
        values[1] = by_rank(0, is_mid * (t0 - old_blocks), 0, 0)
        for k, value in enumerate(values):
            scalars[k] = value

    smem = pl.BlockSpec(memory_space=pltpu.SMEM)
    one = jax.ShapeDtypeStruct((1,), jnp.int32)
    pick, scalars, lane0, lane1 = pl.pallas_call(
        plan,
        in_specs=[smem] * 2,
        out_specs=[smem] * 4,
        out_shape=(one, jax.ShapeDtypeStruct((15,), jnp.int32)) + (one,) * 2,
        name="plan",
    )(ranks, tallies)
    pick, lane0, lane1 = (a.reshape(()) for a in (pick, lane0, lane1))

    def permute(a, pairs):
        return lax.ppermute(a, AXES, pairs)

    tie = lax.optimization_barrier

    def body(v, args):
        scalars, lane0, lane1, x, z, dt, enter, leave, w, ssm, conv, *params = args
        early, relay = split(v)
        second_n = 2 * v - early
        n, k, m = early * UNIT, second_n * UNIT, relay * UNIT
        far_n = n + k - 2 * m

        first = cut_rows(scalars, w, n)
        y1 = permute(first, across)
        scalars, first = tie((scalars, first))
        out_w, side, second, third, partial, states = decode_here(
            scalars, cap, most, (k, far_n), x, z, dt, enter, leave, w, ssm, conv, *params
        )
        y2 = permute(second, across)
        y1, states, partial, side = tie((y1, states, partial, side))
        x1, z1 = permute(y1, along_x), permute(y1, along_z)

        features = partial.shape[1]
        odd = scalars[0] & 1
        core = odd * (features // 2)
        mine = lax.dynamic_slice_in_dim(partial, core, features // 2, 1)
        theirs = lax.dynamic_slice_in_dim(partial, features // 2 - core, features // 2, 1)
        chip_sum = (mine + permute(theirs, cores)).astype(BF)
        total = (chip_sum.astype(F32) + permute(chip_sum, chips).astype(F32)).astype(BF)
        across_s = permute(lax.dynamic_slice_in_dim(states, lane0, v * BLOCK, 1), across)
        side_s = permute(lax.dynamic_slice_in_dim(states, lane1, most * BLOCK, 1), inside)

        y2, x1, z1, side, third, total, across_s, side_s = tie(
            (y2, x1, z1, side, third, total, across_s, side_s)
        )

        y3 = permute(third, across)
        x2, z2 = permute(y2, along_x), permute(y2, along_z)
        side = permute(side, inside)
        to_x, to_z = z1[:m], x1[m : 2 * m]
        x3, z3 = permute(to_x, along_x), permute(to_z, along_z)
        scalars, to_x, to_z = tie((scalars, to_x, to_z))
        other = permute(total, cores)
        decoded = jnp.concatenate(
            [jnp.where(odd == 0, total, other), jnp.where(odd == 0, other, total)], axis=1
        )
        out_w = place_rows(
            scalars,
            out_w,
            [
                (y1, 0, n, lambda q: 2 * v * q),
                (y2, 0, k, lambda q: 2 * v * q + early),
                (x1, 0, n, lambda q: 2 * v * (q ^ 2)),
                (z1, 0, n, lambda q: 2 * v * (q ^ 1)),
            ],
            blanks=True,
        )
        new_ssm, new_conv = place_states(scalars, cap, states, side_s, across_s, ssm.shape[1])
        out_w = place_rows(
            scalars,
            out_w,
            [
                (x2, 0, k, lambda q: 2 * v * (q ^ 2) + early),
                (z2, 0, k, lambda q: 2 * v * (q ^ 1) + early),
            ],
            side,
        )
        out_w = place_rows(
            scalars,
            out_w,
            [
                (x3, 0, m, lambda q: 2 * v * (3 - q)),
                (z3, 0, m, lambda q: 2 * v * (3 - q) + relay),
                (y3, 0, far_n, lambda q: 2 * v * (3 - q) + 2 * relay),
            ],
        )
        return decoded, out_w, new_ssm, new_conv

    args = (scalars, lane0, lane1, x, z, dt, enter, leave, w, ssm, conv, logs, taps, offs, inc, res)
    branches = [lambda args, v=v: body(v, args) for v in range(fewest, old_blocks - 1)]
    decoded, out_w, new_ssm, new_conv = lax.switch(pick, branches, args)
    return decoded.reshape(x.shape[0], x.shape[1], -1), out_w, new_ssm, new_conv.T


def solution(mesh):
    placed = (
        P(None, ("groups", "dp"), "tp"),
        P(None, ("groups", "dp"), "tp"),
        P(None, ("groups", "dp"), "tp"),
        P(None, ("groups", "dp"), None),
        P(None, ("groups", "dp"), None),
        P("tp", None),
        P("tp", ("groups", "dp")),
        P("tp", ("groups", "dp")),
    ) + (P(),) * 7
    square = mesh.shape["tp"] == 4 and mesh.shape["groups"] == 2 and mesh.shape["dp"] % 2 == 0
    return jax.shard_map(
        neighbours if square else general,
        mesh=mesh,
        in_specs=placed,
        out_specs=(
            P(None, ("groups", "dp"), None),
            P(("groups", "tp"), None),
            P("tp", ("groups", "dp")),
            P("tp", ("groups", "dp")),
        ),
        check_vma=False,
    )
```

profile of v0, /device:TPU:1, one launch (start us, length us, event | category | flops | bytes accessed | tf_op | source)
XLA Modules:
  0.0 92.2 jit_solution(2149830928674318057)
XLA Ops:
  0.6 1.3 %plan.1 = (s32[1]{0:T(128)}, s32[15]{0:T(128)S(1)}, s32[1]{0:T(128)}, s32[1]{0:T(128)}) custom-call(s32[3]{0:T(128)} %ranks.1, s32[3]{0:T(128)} %tallies.1), custom_call_target="tpu_custom_call" | custom-call | tf_op jit(solution)/shard_map/plan/pallas_call | solution.py:531
  2.6 88.9 %conditional.1 = (bf16[2944,4096]{1,0:T(8,128)(2,1)}, f32[2944,128]{1,0:T(8,128)}, f32[32,2944]{1,0:T(8,128)}, bf16[4,8,4096]{2,1,0:T(8,128)(2,1)S(1)}) conditional(s32[]{:T(128)} %bitcast.72, (s32[15]{0:T(128)S(1)}, bf16[2048,4096]{1,0:T(8,128)(2,1)}, f32[4,8,16]{2,1,0:T(8,128)}, f32[4,8,16]{2,1,0:T(8,128)}, ...), branch_computations={%region_0.1_spmd, %region_1.2_spmd, %region_2.3_spmd, %region_3.4_... | conditional | flops 1048592 | bytes 128920584 | solution.py:620
  2.7 1.8 %cut_rows.6 = bf16[144,4096]{1,0:T(8,128)(2,1)S(1)} custom-call(s32[15]{0:T(128)S(1)} %get-tuple-element.221.sc, bf16[2048,4096]{1,0:T(8,128)(2,1)} %get-tuple-element.194.w_ref.w_all), custom_call_target="tpu_custom_call" | custom-call | bytes 1024 | tf_op jit(solution)/shard_map/cond/branch_0_fun/cut_rows/pallas_call | solution.py:287
  4.5 4.5 %collective-permute-start.1 = (bf16[144,4096]{1,0:T(8,128)(2,1)S(1)}, bf16[144,4096]{1,0:T(8,128)(2,1)S(1)}, u32[]{:S(2)}, u32[]{:S(2)}) collective-permute-start(bf16[144,4096]{1,0:T(8,128)(2,1)S(1)} %cut_rows.6), channel_id=1, source_target_pairs={{4,8},{8,4},{5,9},{9,5},{6,10},{10,6},{7,11},{11,7},{20,24},{24,20... | collective-permute-start | bytes 3538952 | tf_op jit(solution)/shard_map/cond/branch_0_fun/ppermute | solution.py:541
  9.6 17.8 %decode.6 = (bf16[2944,4096]{1,0:T(8,128)(2,1)}, bf16[896,4096]{1,0:T(8,128)(2,1)}, bf16[144,4096]{1,0:T(8,128)(2,1)}, bf16[160,4096]{1,0:T(8,128)(2,1)}, f32[32...) custom-call(s32[15]{0:T(128)S(1)} %get-tuple-element.221.sc, bf16[4,8,2048]{2,1,0:T(8,128)(2,1)} %get-tuple-element.196.x, ...), custom_call_target="tpu_custom_call" | custom-call | bytes 1024 | tf_op jit(solution)/shard_map/cond/branch_0_fun/decode/pallas_call | solution.py:253
  28.2 1.9 %collective-permute-start = (bf16[144,4096]{1,0:T(8,128)(2,1)}, bf16[144,4096]{1,0:T(8,128)(2,1)S(1)}, u32[]{:S(2)}, u32[]{:S(2)}) collective-permute-start(bf16[144,4096]{1,0:T(8,128)(2,1)} %get-tuple-element.208), channel_id=1, source_target_pairs={{4,8},{8,4},{5,9},{9,5},{6,10},{10,6},{7,11},{11,7},{20,24},{24,20... | collective-permute-start | bytes 3538952 | tf_op jit(solution)/shard_map/cond/branch_0_fun/ppermute | solution.py:541
  33.9 3.3 %collective-permute-start.3 = (bf16[144,4096]{1,0:T(8,128)(2,1)S(1)}, bf16[144,4096]{1,0:T(8,128)(2,1)S(1)}, u32[]{:S(2)}, u32[]{:S(2)}) collective-permute-start(bf16[144,4096]{1,0:T(8,128)(2,1)S(1)} %collective-permute-done.1.refs_0_), channel_id=1, source_target_pairs={{4,5},{8,9},{5,4},{9,8},{6,7},{10,11},{7,6},{11,10},{20,21},{24,25... | collective-permute-start | bytes 3538952 | tf_op jit(solution)/shard_map/cond/branch_0_fun/ppermute | solution.py:541
  37.3 3.1 %collective-permute-start.2 = (bf16[144,4096]{1,0:T(8,128)(2,1)S(1)}, bf16[144,4096]{1,0:T(8,128)(2,1)S(1)}, u32[]{:S(2)}, u32[]{:S(2)}) collective-permute-start(bf16[144,4096]{1,0:T(8,128)(2,1)S(1)} %collective-permute-done.1.refs_0_), channel_id=1, source_target_pairs={{4,20},{8,24},{5,21},{9,25},{6,22},{10,26},{7,23},{11,27},{20,4},{... | collective-permute-start | bytes 3538952 | tf_op jit(solution)/shard_map/cond/branch_0_fun/ppermute | solution.py:541
  40.5 1.3 %collective-permute-start.7 = (bf16[160,896]{1,0:T(8,128)(2,1)S(1)}, bf16[160,896]{1,0:T(8,128)(2,1)S(1)}, u32[]{:S(2)}, u32[]{:S(2)}) collective-permute-start(bf16[160,896]{1,0:T(8,128)(2,1)S(1)} %constant_dynamic-slice_fusion), channel_id=1, source_target_pairs={{4,0},{8,12},{5,1},{9,13},{6,2},{10,14},{7,3},{11,15},{20,16},{24,... | collective-permute-start | bytes 860168 | tf_op jit(solution)/shard_map/cond/branch_0_fun/ppermute | solution.py:541
  43.1 5.4 %collective-permute-done.5 = bf16[32,2048]{1,0:T(8,128)(2,1)S(1)} collective-permute-done((bf16[32,2048]{1,0:T(8,128)(2,1)S(1)}, bf16[32,2048]{1,0:T(8,128)(2,1)S(1)}, u32[]{:S(2)}, u32[]{:S(2)}) %collective-permute-start.5) | collective-permute-done | bytes 131104 | tf_op jit(solution)/shard_map/cond/branch_0_fun/ppermute | solution.py:541
  48.5 3.6 %collective-permute-start.6 = (bf16[160,1152]{1,0:T(8,128)(2,1)S(1)}, bf16[160,1152]{1,0:T(8,128)(2,1)S(1)}, u32[]{:S(2)}, u32[]{:S(2)}) collective-permute-start(bf16[160,1152]{1,0:T(8,128)(2,1)S(1)} %constant_dynamic-slice_fusion.1), channel_id=1, source_target_pairs={{4,8},{8,4},{5,9},{9,5},{6,10},{10,6},{7,11},{11,7},{20,24},{24,20... | collective-permute-start | bytes 1105928 | tf_op jit(solution)/shard_map/cond/branch_0_fun/ppermute | solution.py:541
  52.2 5.2 %collective-permute-done.6.across_ref = bf16[160,1152]{1,0:T(8,128)(2,1)S(1)} collective-permute-done((bf16[160,1152]{1,0:T(8,128)(2,1)S(1)}, bf16[160,1152]{1,0:T(8,128)(2,1)S(1)}, u32[]{:S(2)}, u32[]{:S(2)}) %collective-permute-start.6) | collective-permute-done | bytes 368672 | tf_op jit(solution)/shard_map/cond/branch_0_fun/ppermute | solution.py:541
  57.3 1.8 %collective-permute-start.13 = (bf16[896,4096]{1,0:T(8,128)(2,1)}, bf16[896,4096]{1,0:T(8,128)(2,1)S(1)}, u32[]{:S(2)}, u32[]{:S(2)}) collective-permute-start(bf16[896,4096]{1,0:T(8,128)(2,1)} %get-tuple-element.224), channel_id=1, source_target_pairs={{4,0},{8,12},{5,1},{9,13},{6,2},{10,14},{7,3},{11,15},{20,16},{24,... | collective-permute-start | bytes 22020104 | tf_op jit(solution)/shard_map/cond/branch_0_fun/ppermute | solution.py:541
  59.1 2.0 %collective-permute-start.12 = (bf16[144,4096]{1,0:T(8,128)(2,1)S(1)}, bf16[144,4096]{1,0:T(8,128)(2,1)S(1)}, u32[]{:S(2)}, u32[]{:S(2)}) collective-permute-start(bf16[144,4096]{1,0:T(8,128)(2,1)S(1)} %collective-permute-done.refs_1_), channel_id=1, source_target_pairs={{4,5},{8,9},{5,4},{9,8},{6,7},{10,11},{7,6},{11,10},{20,21},{24,25... | collective-permute-start | bytes 3538952 | tf_op jit(solution)/shard_map/cond/branch_0_fun/ppermute | solution.py:541
  61.1 3.9 %collective-permute-start.10 = (bf16[160,4096]{1,0:T(8,128)(2,1)S(1)}, bf16[160,4096]{1,0:T(8,128)(2,1)S(1)}, u32[]{:S(2)}, u32[]{:S(2)}) collective-permute-start(bf16[160,4096]{1,0:T(8,128)(2,1)S(1)} %copy-done.41), channel_id=1, source_target_pairs={{4,8},{8,4},{5,9},{9,5},{6,10},{10,6},{7,11},{11,7},{20,24},{24,20... | collective-permute-start | bytes 3932168 | tf_op jit(solution)/shard_map/cond/branch_0_fun/ppermute | solution.py:541
  65.1 2.8 %collective-permute-start.11 = (bf16[144,4096]{1,0:T(8,128)(2,1)S(1)}, bf16[144,4096]{1,0:T(8,128)(2,1)S(1)}, u32[]{:S(2)}, u32[]{:S(2)}) collective-permute-start(bf16[144,4096]{1,0:T(8,128)(2,1)S(1)} %collective-permute-done.refs_1_), channel_id=1, source_target_pairs={{4,20},{8,24},{5,21},{9,25},{6,22},{10,26},{7,23},{11,27},{20,4},{... | collective-permute-start | bytes 3538952 | tf_op jit(solution)/shard_map/cond/branch_0_fun/ppermute | solution.py:541
  68.1 4.0 %place_rows.18.refs_3_ = bf16[2944,4096]{1,0:T(8,128)(2,1)} custom-call(s32[15]{0:T(128)S(1)} %get-tuple-element.221.sc, bf16[144,4096]{1,0:T(8,128)(2,1)S(1)} %collective-permute-done.1.refs_0_, bf16[144,4096]{1,0:T(8,128)(2,1)S(1)} %collective-permute-done.refs_1_, ...), custom_call_target="tpu_custom_call", output_to_operand_aliasing={{}: (5, {})} | custom-call | bytes 1024 | tf_op jit(solution)/shard_map/cond/branch_0_fun/place_rows/pallas_call | solution.py:391
  72.1 4.0 %place_states.6 = (f32[2944,128]{1,0:T(8,128)}, f32[32,2944]{1,0:T(8,128)}) custom-call(s32[15]{0:T(128)S(1)} %get-tuple-element.221.sc, bf16[160,2048]{1,0:T(8,128)(2,1)S(1)} %get-tuple-element.216.own_ref, bf16[160,896]{1,0:T(8,128)(2,1)S(1)} %collective-permute-done.7.side_ref, bf16[160,1152]{1,0:T(8,128)(2,1)S(1)} %collective-permute-done.6.across_ref), custom_call_target="tpu_custom_call" | custom-call | bytes 1024 | tf_op jit(solution)/shard_map/cond/branch_0_fun/place_states/pallas_call | solution.py:451
  76.1 2.5 %collective-permute-start.9 = (bf16[64,4096]{1,0:T(8,128)(2,1)S(1)}, bf16[64,4096]{1,0:T(8,128)(2,1)S(1)}, u32[]{:S(2)}, u32[]{:S(2)}) collective-permute-start(bf16[64,4096]{1,0:T(8,128)(2,1)S(1)} %slice.38), channel_id=1, source_target_pairs={{4,5},{8,9},{5,4},{9,8},{6,7},{10,11},{7,6},{11,10},{20,21},{24,25... | collective-permute-start | bytes 1572872 | tf_op jit(solution)/shard_map/cond/branch_0_fun/ppermute | solution.py:541
  78.6 3.1 %collective-permute-start.8 = (bf16[64,4096]{1,0:T(8,128)(2,1)S(1)}, bf16[64,4096]{1,0:T(8,128)(2,1)S(1)}, u32[]{:S(2)}, u32[]{:S(2)}) collective-permute-start(bf16[64,4096]{1,0:T(8,128)(2,1)S(1)} %slice.37), channel_id=1, source_target_pairs={{4,20},{8,24},{5,21},{9,25},{6,22},{10,26},{7,23},{11,27},{20,4},{... | collective-permute-start | bytes 1572872 | tf_op jit(solution)/shard_map/cond/branch_0_fun/ppermute | solution.py:541
  82.0 2.8 %place_rows.19.refs_3_ = bf16[2944,4096]{1,0:T(8,128)(2,1)} custom-call(s32[15]{0:T(128)S(1)} %get-tuple-element.221.sc, bf16[144,4096]{1,0:T(8,128)(2,1)S(1)} %collective-permute-done.11.refs_0_, bf16[144,4096]{1,0:T(8,128)(2,1)S(1)} %collective-permute-done.12.refs_1_, ...), custom_call_target="tpu_custom_call", output_to_operand_aliasing={{}: (4, {})} | custom-call | bytes 1024 | tf_op jit(solution)/shard_map/cond/branch_0_fun/place_rows/pallas_call | solution.py:391
  84.8 1.2 %collective-permute-done.9.refs_1_ = bf16[64,4096]{1,0:T(8,128)(2,1)S(1)} collective-permute-done((bf16[64,4096]{1,0:T(8,128)(2,1)S(1)}, bf16[64,4096]{1,0:T(8,128)(2,1)S(1)}, u32[]{:S(2)}, u32[]{:S(2)}) %collective-permute-start.9) | collective-permute-done | bytes 524320 | tf_op jit(solution)/shard_map/cond/branch_0_fun/ppermute | solution.py:541
  86.0 2.5 %collective-permute-done.8.refs_0_ = bf16[64,4096]{1,0:T(8,128)(2,1)S(1)} collective-permute-done((bf16[64,4096]{1,0:T(8,128)(2,1)S(1)}, bf16[64,4096]{1,0:T(8,128)(2,1)S(1)}, u32[]{:S(2)}, u32[]{:S(2)}) %collective-permute-start.8) | collective-permute-done | bytes 524320 | tf_op jit(solution)/shard_map/cond/branch_0_fun/ppermute | solution.py:541
  88.6 2.4 %place_rows.20 = bf16[2944,4096]{1,0:T(8,128)(2,1)} custom-call(s32[15]{0:T(128)S(1)} %get-tuple-element.221.sc, bf16[64,4096]{1,0:T(8,128)(2,1)S(1)} %collective-permute-done.8.refs_0_, bf16[64,4096]{1,0:T(8,128)(2,1)S(1)} %collective-permute-done.9.refs_1_, bf16[160,4096]{1,0:T(8,128)(2,1)S(1)} %collective-permute-done.10.refs_2_, ...), custom_call_target="tpu_custom_call", output_to_operand_aliasing={{}: (4, {})} | custom-call | bytes 1024 | tf_op jit(solution)/shard_map/cond/branch_0_fun/place_rows/pallas_call | solution.py:391
  (39 shorter events, 3.8 us)
Async XLA Ops:
  2.6 6.4 %copy-start.18 = (f32[2048,32]{0,1:T(8,128)S(1)}, f32[2048,32]{0,1:T(8,128)}, u32[]{:S(2)}) copy-start(f32[2048,32]{0,1:T(8,128)} %get-tuple-element.202) | copy-start | bytes 786436 | tf_op jit(solution)/shard_map/cond
  2.6 6.7 %copy-start.28 = (f32[4,8,16]{2,1,0:T(8,128)S(1)}, f32[4,8,16]{2,1,0:T(8,128)}, u32[]{:S(2)}) copy-start(f32[4,8,16]{2,1,0:T(8,128)} %get-tuple-element.199) | copy-start | bytes 6148 | tf_op jit(solution)/shard_map/cond
  2.7 6.8 %copy-start.32 = (f32[4,8,16]{2,1,0:T(8,128)S(1)}, f32[4,8,16]{2,1,0:T(8,128)}, u32[]{:S(2)}) copy-start(f32[4,8,16]{2,1,0:T(8,128)} %get-tuple-element.200) | copy-start | bytes 6148 | tf_op jit(solution)/shard_map/cond
  4.5 23.0 %collective-permute-start.1 = (bf16[144,4096]{1,0:T(8,128)(2,1)S(1)}, bf16[144,4096]{1,0:T(8,128)(2,1)S(1)}, u32[]{:S(2)}, u32[]{:S(2)}) collective-permute-start(bf16[144,4096]{1,0:T(8,128)(2,1)S(1)} %cut_rows.6), channel_id=1, source_target_pairs={{4,8},{8,4},{5,9},{9,5},{6,10},{10,6},{7,11},{11,7},{20,24},{24,20... | collective-permute-start | bytes 3538952 | tf_op jit(solution)/shard_map/cond/branch_0_fun/ppermute | solution.py:541
  27.4 0.8 copy-start.9
  27.5 14.4 %collective-permute-start.4 = (f32[32,2048]{1,0:T(8,128)S(1)}, f32[32,2048]{1,0:T(8,128)S(1)}, u32[]{:S(2)}, u32[]{:S(2)}) collective-permute-start(f32[32,2048]{1,0:T(8,128)S(1)} %constant_dynamic-slice_fusion.2), channel_id=1, source_target_pairs={{0,4},{4,0},{8,12},{12,8},{1,5},{5,1},{9,13},{13,9},{2,6},{6,2},{1... | collective-permute-start | bytes 786440 | tf_op jit(solution)/shard_map/cond/branch_0_fun/ppermute | solution.py:541
  28.2 23.9 %collective-permute-start = (bf16[144,4096]{1,0:T(8,128)(2,1)}, bf16[144,4096]{1,0:T(8,128)(2,1)S(1)}, u32[]{:S(2)}, u32[]{:S(2)}) collective-permute-start(bf16[144,4096]{1,0:T(8,128)(2,1)} %get-tuple-element.208), channel_id=1, source_target_pairs={{4,8},{8,4},{5,9},{9,5},{6,10},{10,6},{7,11},{11,7},{20,24},{24,20... | collective-permute-start | bytes 3538952 | tf_op jit(solution)/shard_map/cond/branch_0_fun/ppermute | solution.py:541
  33.9 27.2 %copy-start.41 = (bf16[160,4096]{1,0:T(8,128)(2,1)S(1)}, bf16[160,4096]{1,0:T(8,128)(2,1)}, u32[]{:S(2)}) copy-start(bf16[160,4096]{1,0:T(8,128)(2,1)} %get-tuple-element.222) | copy-start | bytes 3932164 | tf_op jit(solution)/shard_map/cond
  33.9 23.4 %collective-permute-start.3 = (bf16[144,4096]{1,0:T(8,128)(2,1)S(1)}, bf16[144,4096]{1,0:T(8,128)(2,1)S(1)}, u32[]{:S(2)}, u32[]{:S(2)}) collective-permute-start(bf16[144,4096]{1,0:T(8,128)(2,1)S(1)} %collective-permute-done.1.refs_0_), channel_id=1, source_target_pairs={{4,5},{8,9},{5,4},{9,8},{6,7},{10,11},{7,6},{11,10},{20,21},{24,25... | collective-permute-start | bytes 3538952 | tf_op jit(solution)/shard_map/cond/branch_0_fun/ppermute | solution.py:541
  37.3 20.1 %collective-permute-start.2 = (bf16[144,4096]{1,0:T(8,128)(2,1)S(1)}, bf16[144,4096]{1,0:T(8,128)(2,1)S(1)}, u32[]{:S(2)}, u32[]{:S(2)}) collective-permute-start(bf16[144,4096]{1,0:T(8,128)(2,1)S(1)} %collective-permute-done.1.refs_0_), channel_id=1, source_target_pairs={{4,20},{8,24},{5,21},{9,25},{6,22},{10,26},{7,23},{11,27},{20,4},{... | collective-permute-start | bytes 3538952 | tf_op jit(solution)/shard_map/cond/branch_0_fun/ppermute | solution.py:541
  40.5 11.6 %collective-permute-start.7 = (bf16[160,896]{1,0:T(8,128)(2,1)S(1)}, bf16[160,896]{1,0:T(8,128)(2,1)S(1)}, u32[]{:S(2)}, u32[]{:S(2)}) collective-permute-start(bf16[160,896]{1,0:T(8,128)(2,1)S(1)} %constant_dynamic-slice_fusion), channel_id=1, source_target_pairs={{4,0},{8,12},{5,1},{9,13},{6,2},{10,14},{7,3},{11,15},{20,16},{24,... | collective-permute-start | bytes 860168 | tf_op jit(solution)/shard_map/cond/branch_0_fun/ppermute | solution.py:541
  42.9 5.6 %collective-permute-start.5 = (bf16[32,2048]{1,0:T(8,128)(2,1)S(1)}, bf16[32,2048]{1,0:T(8,128)(2,1)S(1)}, u32[]{:S(2)}, u32[]{:S(2)}) collective-permute-start(bf16[32,2048]{1,0:T(8,128)(2,1)S(1)} %add_convert_fusion.1), channel_id=1, source_target_pairs={{0,8},{4,12},{8,0},{12,4},{1,9},{5,13},{9,1},{13,5},{2,10},{6,14},... | collective-permute-start | bytes 393224 | tf_op jit(solution)/shard_map/cond/branch_0_fun/ppermute | solution.py:541
  48.5 8.8 %collective-permute-start.6 = (bf16[160,1152]{1,0:T(8,128)(2,1)S(1)}, bf16[160,1152]{1,0:T(8,128)(2,1)S(1)}, u32[]{:S(2)}, u32[]{:S(2)}) collective-permute-start(bf16[160,1152]{1,0:T(8,128)(2,1)S(1)} %constant_dynamic-slice_fusion.1), channel_id=1, source_target_pairs={{4,8},{8,4},{5,9},{9,5},{6,10},{10,6},{7,11},{11,7},{20,24},{24,20... | collective-permute-start | bytes 1105928 | tf_op jit(solution)/shard_map/cond/branch_0_fun/ppermute | solution.py:541
  57.3 24.7 %collective-permute-start.13 = (bf16[896,4096]{1,0:T(8,128)(2,1)}, bf16[896,4096]{1,0:T(8,128)(2,1)S(1)}, u32[]{:S(2)}, u32[]{:S(2)}) collective-permute-start(bf16[896,4096]{1,0:T(8,128)(2,1)} %get-tuple-element.224), channel_id=1, source_target_pairs={{4,0},{8,12},{5,1},{9,13},{6,2},{10,14},{7,3},{11,15},{20,16},{24,... | collective-permute-start | bytes 22020104 | tf_op jit(solution)/shard_map/cond/branch_0_fun/ppermute | solution.py:541
  59.1 19.5 %collective-permute-start.12 = (bf16[144,4096]{1,0:T(8,128)(2,1)S(1)}, bf16[144,4096]{1,0:T(8,128)(2,1)S(1)}, u32[]{:S(2)}, u32[]{:S(2)}) collective-permute-start(bf16[144,4096]{1,0:T(8,128)(2,1)S(1)} %collective-permute-done.refs_1_), channel_id=1, source_target_pairs={{4,5},{8,9},{5,4},{9,8},{6,7},{10,11},{7,6},{11,10},{20,21},{24,25... | collective-permute-start | bytes 3538952 | tf_op jit(solution)/shard_map/cond/branch_0_fun/ppermute | solution.py:541
  61.1 27.4 %collective-permute-start.10 = (bf16[160,4096]{1,0:T(8,128)(2,1)S(1)}, bf16[160,4096]{1,0:T(8,128)(2,1)S(1)}, u32[]{:S(2)}, u32[]{:S(2)}) collective-permute-start(bf16[160,4096]{1,0:T(8,128)(2,1)S(1)} %copy-done.41), channel_id=1, source_target_pairs={{4,8},{8,4},{5,9},{9,5},{6,10},{10,6},{7,11},{11,7},{20,24},{24,20... | collective-permute-start | bytes 3932168 | tf_op jit(solution)/shard_map/cond/branch_0_fun/ppermute | solution.py:541
  65.1 16.9 %collective-permute-start.11 = (bf16[144,4096]{1,0:T(8,128)(2,1)S(1)}, bf16[144,4096]{1,0:T(8,128)(2,1)S(1)}, u32[]{:S(2)}, u32[]{:S(2)}) collective-permute-start(bf16[144,4096]{1,0:T(8,128)(2,1)S(1)} %collective-permute-done.refs_1_), channel_id=1, source_target_pairs={{4,20},{8,24},{5,21},{9,25},{6,22},{10,26},{7,23},{11,27},{20,4},{... | collective-permute-start | bytes 3538952 | tf_op jit(solution)/shard_map/cond/branch_0_fun/ppermute | solution.py:541
  67.9 8.2 %collective-permute-start.14 = (bf16[32,2048]{1,0:T(8,128)(2,1)S(1)}, bf16[32,2048]{1,0:T(8,128)(2,1)S(1)}, u32[]{:S(2)}, u32[]{:S(2)}) collective-permute-start(bf16[32,2048]{1,0:T(8,128)(2,1)S(1)} %add_convert_fusion), channel_id=1, source_target_pairs={{0,4},{4,0},{8,12},{12,8},{1,5},{5,1},{9,13},{13,9},{2,6},{6,2},{1... | collective-permute-start | bytes 393224 | tf_op jit(solution)/shard_map/cond/branch_0_fun/ppermute | solution.py:541
  76.1 9.9 %collective-permute-start.9 = (bf16[64,4096]{1,0:T(8,128)(2,1)S(1)}, bf16[64,4096]{1,0:T(8,128)(2,1)S(1)}, u32[]{:S(2)}, u32[]{:S(2)}) collective-permute-start(bf16[64,4096]{1,0:T(8,128)(2,1)S(1)} %slice.38), channel_id=1, source_target_pairs={{4,5},{8,9},{5,4},{9,8},{6,7},{10,11},{7,6},{11,10},{20,21},{24,25... | collective-permute-start | bytes 1572872 | tf_op jit(solution)/shard_map/cond/branch_0_fun/ppermute | solution.py:541
  78.6 9.9 %collective-permute-start.8 = (bf16[64,4096]{1,0:T(8,128)(2,1)S(1)}, bf16[64,4096]{1,0:T(8,128)(2,1)S(1)}, u32[]{:S(2)}, u32[]{:S(2)}) collective-permute-start(bf16[64,4096]{1,0:T(8,128)(2,1)S(1)} %slice.37), channel_id=1, source_target_pairs={{4,20},{8,24},{5,21},{9,25},{6,22},{10,26},{7,23},{11,27},{20,4},{... | collective-permute-start | bytes 1572872 | tf_op jit(solution)/shard_map/cond/branch_0_fun/ppermute | solution.py:541
  91.5 0.7 copy-start.36
where the time goes:
time: 93.4 us; the launch traced here: 92.2 us
  starting transfers between devices  34.2 us (37%)
  Pallas kernels  34.1 us (37%)
  waiting for transfers between devices  14.5 us (16%)
  loops' own time  4.7 us (5%)
  local copies, waits for them, and re-layouts  2.3 us (2%)
  between operations  1.3 us (1%)
  other arithmetic  1.07 us (1%)
    ppermute x15, starting transfers between devices, permute(): return lax.ppermute(a, AXES, pairs)  34.2 us
    pallas_call x1, Pallas kernels, decode_here(): pl.pallas_call(decode_kernel, grid_spec=grid_spec, out_shape=(jax.ShapeDt...  17.8 us
    ppermute x15, waiting for transfers between devices, permute(): return lax.ppermute(a, AXES, pairs)  14.5 us
    pallas_call x3, Pallas kernels, place_rows(): pl.pallas_call(kernel, grid_spec=pltpu.PrefetchScalarGridSpec(num_scalar_...  9.22 us
    another operation x1, loops' own time, neighbours(): decoded, out_w, new_ssm, new_conv = lax.switch(pick, branches, args)  4.7 us
    pallas_call x1, Pallas kernels, place_states(): pl.pallas_call(kernel, grid_spec=pltpu.PrefetchScalarGridSpec(num_scalar_...  3.96 us
  transfers between devices with their start and end apart: 15, of which 5 were waited for; matrix products, arithmetic and copies ran while one was open for 2% of the time, Pallas kernels for 31%

commit v1 on v0

--- a/solution.py
+++ b/solution.py
@@ -468,7 +468,7 @@
 
 
 def split(blocks):
-    return blocks, (5 * blocks + 5) // 11
+    return blocks, (3 * blocks + 5) // 11
 
 
 def neighbours(x, z, dt, enter, leave, w, ssm, conv, logs, taps, offs, inc, res, ranks, tallies):

time: 93.4 us -> 102 us (1.092); the launches traced: 92.2 us -> 102 us
  starting transfers between devices: 34.2 us -> 39.4 us
  waiting for transfers between devices: 14.5 us -> 17.4 us
    ppermute x15, starting transfers between devices: 34.2 us -> 39.4 us  [permute(): return lax.ppermute(a, AXES, pairs)]
    ppermute x15, waiting for transfers between devices: 14.5 us -> 17.4 us  [permute(): return lax.ppermute(a, AXES, pairs)]
    pallas_call x1, Pallas kernels: 3.96 us -> 1.95 us  [place_states(): pl.pallas_call(kernel, grid_spec=pltpu.PrefetchScalarGridSpec(num_scalar_...]
    pallas_call x3, Pallas kernels: 9.22 us -> 10.7 us  [place_rows(): pl.pallas_call(kernel, grid_spec=pltpu.PrefetchScalarGridSpec(num_scalar_...]
    pallas_call x1, Pallas kernels: 1.82 us -> 3.27 us  [cut_rows(): pl.pallas_call(kernel, grid_spec=pltpu.PrefetchScalarGridSpec(num_scalar_...]
    slice x2, local copies, waits for them, and re-layouts: 0.07 us -> 1.11 us  [body(): to_x, to_z = (z1[:m], x1[m:2 * m])]
  transfers between devices with their start and end apart: 15 -> 15, of which waited for: 5 -> 8; matrix products, arithmetic and copies ran while one was open for 2% -> 3% of each run, Pallas kernels for 31% -> 29%
where the time goes in v1:
time: 102 us
  starting transfers between devices  39.4 us (39%)
  Pallas kernels  34.9 us (34%)
  waiting for transfers between devices  17.4 us (17%)
  loops' own time  4.89 us (5%)
  local copies, waits for them, and re-layouts  3.26 us (3%)
  between operations  1.51 us (1%)
    ppermute x15, starting transfers between devices, permute(): return lax.ppermute(a, AXES, pairs)  39.4 us
    pallas_call x1, Pallas kernels, decode_here(): pl.pallas_call(decode_kernel, grid_spec=grid_spec, out_shape=(jax.ShapeDt...  17.7 us
    ppermute x15, waiting for transfers between devices, permute(): return lax.ppermute(a, AXES, pairs)  17.4 us
    pallas_call x3, Pallas kernels, place_rows(): pl.pallas_call(kernel, grid_spec=pltpu.PrefetchScalarGridSpec(num_scalar_...  10.7 us
    another operation x1, loops' own time, neighbours(): decoded, out_w, new_ssm, new_conv = lax.switch(pick, branches, args)  4.89 us
    pallas_call x1, Pallas kernels, cut_rows(): pl.pallas_call(kernel, grid_spec=pltpu.PrefetchScalarGridSpec(num_scalar_...  3.27 us
  transfers between devices with their start and end apart: 15, of which 8 were waited for; matrix products, arithmetic and copies ran while one was open for 3% of the time, Pallas kernels for 29%

profile of v1, /device:TPU:1, one launch (start us, length us, event | category | flops | bytes accessed | tf_op | source)
XLA Modules:
  0.0 102.1 jit_solution(15113395505876626498)
XLA Ops:
  0.6 1.3 %plan.1 = (s32[1]{0:T(128)}, s32[15]{0:T(128)S(1)}, s32[1]{0:T(128)}, s32[1]{0:T(128)}) custom-call(s32[3]{0:T(128)} %ranks.1, s32[3]{0:T(128)} %tallies.1), custom_call_target="tpu_custom_call" | custom-call | tf_op jit(solution)/shard_map/plan/pallas_call | solution.py:531
  2.6 99.3 %conditional.1 = (bf16[2944,4096]{1,0:T(8,128)(2,1)}, f32[2944,128]{1,0:T(8,128)}, f32[32,2944]{1,0:T(8,128)}, bf16[4,8,4096]{2,1,0:T(8,128)(2,1)}) conditional(s32[]{:T(128)} %bitcast.72, (s32[15]{0:T(128)S(1)}, bf16[2048,4096]{1,0:T(8,128)(2,1)}, f32[4,8,16]{2,1,0:T(8,128)}, f32[4,8,16]{2,1,0:T(8,128)}, ...), branch_computations={%region_0.1_spmd, %region_1.2_spmd, %region_2.3_spmd, %region_3.4_... | conditional | flops 1048592 | bytes 129969160 | solution.py:620
  2.9 3.3 %cut_rows.11 = bf16[224,4096]{1,0:T(8,128)(2,1)} custom-call(s32[15]{0:T(128)S(1)} %get-tuple-element.411.sc, bf16[2048,4096]{1,0:T(8,128)(2,1)} %get-tuple-element.384.w_ref.w_all), custom_call_target="tpu_custom_call" | custom-call | bytes 1024 | tf_op jit(solution)/shard_map/cond/branch_5_fun/cut_rows/pallas_call | solution.py:287
  6.2 4.7 %collective-permute-start.76 = (bf16[224,4096]{1,0:T(8,128)(2,1)}, bf16[224,4096]{1,0:T(8,128)(2,1)S(1)}, u32[]{:S(2)}, u32[]{:S(2)}) collective-permute-start(bf16[224,4096]{1,0:T(8,128)(2,1)} %cut_rows.11), channel_id=1, source_target_pairs={{4,8},{8,4},{5,9},{9,5},{6,10},{10,6},{7,11},{11,7},{20,24},{24,20... | collective-permute-start | bytes 5505032 | tf_op jit(solution)/shard_map/cond/branch_5_fun/ppermute | solution.py:541
  11.4 17.7 %decode.11 = (bf16[2944,4096]{1,0:T(8,128)(2,1)}, bf16[896,4096]{1,0:T(8,128)(2,1)}, bf16[224,4096]{1,0:T(8,128)(2,1)}, bf16[320,4096]{1,0:T(8,128)(2,1)}, f32[3...) custom-call(s32[15]{0:T(128)S(1)} %get-tuple-element.411.sc, bf16[4,8,2048]{2,1,0:T(8,128)(2,1)} %get-tuple-element.386.x, ...), custom_call_target="tpu_custom_call" | custom-call | bytes 1024 | tf_op jit(solution)/shard_map/cond/branch_5_fun/decode/pallas_call | solution.py:253
  29.1 2.6 %collective-permute-start.75 = (bf16[224,4096]{1,0:T(8,128)(2,1)}, bf16[224,4096]{1,0:T(8,128)(2,1)}, u32[]{:S(2)}, u32[]{:S(2)}) collective-permute-start(bf16[224,4096]{1,0:T(8,128)(2,1)} %get-tuple-element.398), channel_id=1, source_target_pairs={{4,8},{8,4},{5,9},{9,5},{6,10},{10,6},{7,11},{11,7},{20,24},{24,20... | collective-permute-start | bytes 5505032 | tf_op jit(solution)/shard_map/cond/branch_5_fun/ppermute | solution.py:541
  32.0 1.2 %copy-done = bf16[224,4096]{1,0:T(8,128)(2,1)} copy-done((bf16[224,4096]{1,0:T(8,128)(2,1)}, bf16[224,4096]{1,0:T(8,128)(2,1)S(1)}, u32[]{:S(2)}) %copy-start) | copy-done | bytes 1835032 | tf_op jit(solution)/shard_map/cond
  33.2 3.2 %collective-permute-start.78 = (bf16[224,4096]{1,0:T(8,128)(2,1)}, bf16[224,4096]{1,0:T(8,128)(2,1)S(1)}, u32[]{:S(2)}, u32[]{:S(2)}) collective-permute-start(bf16[224,4096]{1,0:T(8,128)(2,1)} %copy-done), channel_id=1, source_target_pairs={{4,5},{8,9},{5,4},{9,8},{6,7},{10,11},{7,6},{11,10},{20,21},{24,25... | collective-permute-start | bytes 5505032 | tf_op jit(solution)/shard_map/cond/branch_5_fun/ppermute | solution.py:541
  36.4 3.4 %collective-permute-start.77 = (bf16[224,4096]{1,0:T(8,128)(2,1)}, bf16[224,4096]{1,0:T(8,128)(2,1)}, u32[]{:S(2)}, u32[]{:S(2)}) collective-permute-start(bf16[224,4096]{1,0:T(8,128)(2,1)} %copy-done), channel_id=1, source_target_pairs={{4,20},{8,24},{5,21},{9,25},{6,22},{10,26},{7,23},{11,27},{20,4},{... | collective-permute-start | bytes 5505032 | tf_op jit(solution)/shard_map/cond/branch_5_fun/ppermute | solution.py:541
  44.0 2.5 %collective-permute-start.80 = (bf16[32,2048]{1,0:T(8,128)(2,1)S(1)}, bf16[32,2048]{1,0:T(8,128)(2,1)S(1)}, u32[]{:S(2)}, u32[]{:S(2)}) collective-permute-start(bf16[32,2048]{1,0:T(8,128)(2,1)S(1)} %add_convert_fusion.11), channel_id=1, source_target_pairs={{0,8},{4,12},{8,0},{12,4},{1,9},{5,13},{9,1},{13,5},{2,10},{6,14},... | collective-permute-start | bytes 393224 | tf_op jit(solution)/shard_map/cond/branch_5_fun/ppermute | solution.py:541
  46.7 2.1 %collective-permute-start.81 = (bf16[160,1792]{1,0:T(8,128)(2,1)S(1)}, bf16[160,1792]{1,0:T(8,128)(2,1)S(1)}, u32[]{:S(2)}, u32[]{:S(2)}) collective-permute-start(bf16[160,1792]{1,0:T(8,128)(2,1)S(1)} %constant_dynamic-slice_fusion.16), channel_id=1, source_target_pairs={{4,8},{8,4},{5,9},{9,5},{6,10},{10,6},{7,11},{11,7},{20,24},{24,20... | collective-permute-start | bytes 1720328 | tf_op jit(solution)/shard_map/cond/branch_5_fun/ppermute | solution.py:541
  48.9 5.9 %collective-permute-done.80 = bf16[32,2048]{1,0:T(8,128)(2,1)S(1)} collective-permute-done((bf16[32,2048]{1,0:T(8,128)(2,1)S(1)}, bf16[32,2048]{1,0:T(8,128)(2,1)S(1)}, u32[]{:S(2)}, u32[]{:S(2)}) %collective-permute-start.80) | collective-permute-done | bytes 131104 | tf_op jit(solution)/shard_map/cond/branch_5_fun/ppermute | solution.py:541
  54.9 4.4 %collective-permute-start.82 = (bf16[160,896]{1,0:T(8,128)(2,1)S(1)}, bf16[160,896]{1,0:T(8,128)(2,1)S(1)}, u32[]{:S(2)}, u32[]{:S(2)}) collective-permute-start(bf16[160,896]{1,0:T(8,128)(2,1)S(1)} %constant_dynamic-slice_fusion.15), channel_id=1, source_target_pairs={{4,0},{8,12},{5,1},{9,13},{6,2},{10,14},{7,3},{11,15},{20,16},{24,... | collective-permute-start | bytes 860168 | tf_op jit(solution)/shard_map/cond/branch_5_fun/ppermute | solution.py:541
  60.4 2.4 %collective-permute-done.81.across_ref = bf16[160,1792]{1,0:T(8,128)(2,1)S(1)} collective-permute-done((bf16[160,1792]{1,0:T(8,128)(2,1)S(1)}, bf16[160,1792]{1,0:T(8,128)(2,1)S(1)}, u32[]{:S(2)}, u32[]{:S(2)}) %collective-permute-start.81) | collective-permute-done | bytes 573472 | tf_op jit(solution)/shard_map/cond/branch_5_fun/ppermute | solution.py:541
  62.8 1.8 %collective-permute-start.88 = (bf16[896,4096]{1,0:T(8,128)(2,1)}, bf16[896,4096]{1,0:T(8,128)(2,1)S(1)}, u32[]{:S(2)}, u32[]{:S(2)}) collective-permute-start(bf16[896,4096]{1,0:T(8,128)(2,1)} %get-tuple-element.414), channel_id=1, source_target_pairs={{4,0},{8,12},{5,1},{9,13},{6,2},{10,14},{7,3},{11,15},{20,16},{24,... | collective-permute-start | bytes 22020104 | tf_op jit(solution)/shard_map/cond/branch_5_fun/ppermute | solution.py:541
  64.6 3.2 %collective-permute-start.87 = (bf16[224,4096]{1,0:T(8,128)(2,1)}, bf16[224,4096]{1,0:T(8,128)(2,1)S(1)}, u32[]{:S(2)}, u32[]{:S(2)}) collective-permute-start(bf16[224,4096]{1,0:T(8,128)(2,1)} %collective-permute-done.75.refs_1_), channel_id=1, source_target_pairs={{4,5},{8,9},{5,4},{9,8},{6,7},{10,11},{7,6},{11,10},{20,21},{24,25... | collective-permute-start | bytes 5505032 | tf_op jit(solution)/shard_map/cond/branch_5_fun/ppermute | solution.py:541
  67.8 2.9 %collective-permute-start.85 = (bf16[320,4096]{1,0:T(8,128)(2,1)S(1)}, bf16[320,4096]{1,0:T(8,128)(2,1)S(1)}, u32[]{:S(2)}, u32[]{:S(2)}) collective-permute-start(bf16[320,4096]{1,0:T(8,128)(2,1)S(1)} %copy-done.36), channel_id=1, source_target_pairs={{4,8},{8,4},{5,9},{9,5},{6,10},{10,6},{7,11},{11,7},{20,24},{24,20... | collective-permute-start | bytes 7864328 | tf_op jit(solution)/shard_map/cond/branch_5_fun/ppermute | solution.py:541
  70.7 3.1 %collective-permute-start.86 = (bf16[224,4096]{1,0:T(8,128)(2,1)}, bf16[224,4096]{1,0:T(8,128)(2,1)S(1)}, u32[]{:S(2)}, u32[]{:S(2)}) collective-permute-start(bf16[224,4096]{1,0:T(8,128)(2,1)} %collective-permute-done.75.refs_1_), channel_id=1, source_target_pairs={{4,20},{8,24},{5,21},{9,25},{6,22},{10,26},{7,23},{11,27},{20,4},{... | collective-permute-start | bytes 5505032 | tf_op jit(solution)/shard_map/cond/branch_5_fun/ppermute | solution.py:541
  75.0 8.9 %place_rows.33.refs_3_ = bf16[2944,4096]{1,0:T(8,128)(2,1)} custom-call(s32[15]{0:T(128)S(1)} %get-tuple-element.411.sc, bf16[224,4096]{1,0:T(8,128)(2,1)S(1)} %copy-done.1, bf16[224,4096]{1,0:T(8,128)(2,1)} %collective-permute-done.75.refs_1_, bf16[224,4096]{1,0:T(8,128)(2,1)} %collective-permute-done.77.refs_2_, ...), custom_call_target="tpu_custom_call", output_to_operand_aliasing={{}: (5, {})} | custom-call | bytes 1024 | tf_op jit(solution)/shard_map/cond/branch_5_fun/place_rows/pallas_call | solution.py:391
  83.9 1.9 %place_states.11 = (f32[2944,128]{1,0:T(8,128)}, f32[32,2944]{1,0:T(8,128)}) custom-call(s32[15]{0:T(128)S(1)} %get-tuple-element.411.sc, bf16[160,2048]{1,0:T(8,128)(2,1)S(1)} %get-tuple-element.406.own_ref, bf16[160,896]{1,0:T(8,128)(2,1)S(1)} %collective-permute-done.82.side_ref, bf16[160,1792]{1,0:T(8,128)(2,1)S(1)} %collective-permute-done.81.across_ref), custom_call_target="tpu_custom_call" | custom-call | bytes 1024 | tf_op jit(solution)/shard_map/cond/branch_5_fun/place_states/pallas_call | solution.py:451
  85.9 2.4 %collective-permute-start.84 = (bf16[64,4096]{1,0:T(8,128)(2,1)S(1)}, bf16[64,4096]{1,0:T(8,128)(2,1)S(1)}, u32[]{:S(2)}, u32[]{:S(2)}) collective-permute-start(bf16[64,4096]{1,0:T(8,128)(2,1)S(1)} %slice.53), channel_id=1, source_target_pairs={{4,5},{8,9},{5,4},{9,8},{6,7},{10,11},{7,6},{11,10},{20,21},{24,25... | collective-permute-start | bytes 1572872 | tf_op jit(solution)/shard_map/cond/branch_5_fun/ppermute | solution.py:541
  88.8 3.1 %collective-permute-start.83 = (bf16[64,4096]{1,0:T(8,128)(2,1)S(1)}, bf16[64,4096]{1,0:T(8,128)(2,1)S(1)}, u32[]{:S(2)}, u32[]{:S(2)}) collective-permute-start(bf16[64,4096]{1,0:T(8,128)(2,1)S(1)} %slice.52), channel_id=1, source_target_pairs={{4,20},{8,24},{5,21},{9,25},{6,22},{10,26},{7,23},{11,27},{20,4},{... | collective-permute-start | bytes 1572872 | tf_op jit(solution)/shard_map/cond/branch_5_fun/ppermute | solution.py:541
  92.6 2.2 %collective-permute-done.86.refs_0_ = bf16[224,4096]{1,0:T(8,128)(2,1)S(1)} collective-permute-done((bf16[224,4096]{1,0:T(8,128)(2,1)}, bf16[224,4096]{1,0:T(8,128)(2,1)S(1)}, u32[]{:S(2)}, u32[]{:S(2)}) %collective-permute-start.86) | collective-permute-done | bytes 1835040 | tf_op jit(solution)/shard_map/cond/branch_5_fun/ppermute | solution.py:541
  95.8 4.6 %collective-permute-done.83.refs_0_ = bf16[64,4096]{1,0:T(8,128)(2,1)S(1)} collective-permute-done((bf16[64,4096]{1,0:T(8,128)(2,1)S(1)}, bf16[64,4096]{1,0:T(8,128)(2,1)S(1)}, u32[]{:S(2)}, u32[]{:S(2)}) %collective-permute-start.83) | collective-permute-done | bytes 524320 | tf_op jit(solution)/shard_map/cond/branch_5_fun/ppermute | solution.py:541
  (41 shorter events, 6.9 us)
Async XLA Ops:
  2.9 8.0 %copy-start.19 = (f32[2048,32]{0,1:T(8,128)S(1)}, f32[2048,32]{0,1:T(8,128)}, u32[]{:S(2)}) copy-start(f32[2048,32]{0,1:T(8,128)} %get-tuple-element.392) | copy-start | bytes 786436 | tf_op jit(solution)/shard_map/cond
  2.9 8.2 %copy-start.29 = (f32[4,8,16]{2,1,0:T(8,128)S(1)}, f32[4,8,16]{2,1,0:T(8,128)}, u32[]{:S(2)}) copy-start(f32[4,8,16]{2,1,0:T(8,128)} %get-tuple-element.389) | copy-start | bytes 6148 | tf_op jit(solution)/shard_map/cond
  2.9 8.4 %copy-start.35 = (f32[4,8,16]{2,1,0:T(8,128)S(1)}, f32[4,8,16]{2,1,0:T(8,128)}, u32[]{:S(2)}) copy-start(f32[4,8,16]{2,1,0:T(8,128)} %get-tuple-element.390) | copy-start | bytes 6148 | tf_op jit(solution)/shard_map/cond
  6.2 5.2 %copy-start.13 = (f32[8192,16]{0,1:T(8,128)S(1)}, f32[8192,16]{0,1:T(8,128)}, u32[]{:S(2)}) copy-start(f32[8192,16]{0,1:T(8,128)} %get-tuple-element.393) | copy-start | bytes 1572868 | tf_op jit(solution)/shard_map/cond
  6.2 25.8 %collective-permute-start.76 = (bf16[224,4096]{1,0:T(8,128)(2,1)}, bf16[224,4096]{1,0:T(8,128)(2,1)S(1)}, u32[]{:S(2)}, u32[]{:S(2)}) collective-permute-start(bf16[224,4096]{1,0:T(8,128)(2,1)} %cut_rows.11), channel_id=1, source_target_pairs={{4,8},{8,4},{5,9},{9,5},{6,10},{10,6},{7,11},{11,7},{20,24},{24,20... | collective-permute-start | bytes 5505032 | tf_op jit(solution)/shard_map/cond/branch_5_fun/ppermute | solution.py:541
  29.1 30.2 %collective-permute-start.75 = (bf16[224,4096]{1,0:T(8,128)(2,1)}, bf16[224,4096]{1,0:T(8,128)(2,1)}, u32[]{:S(2)}, u32[]{:S(2)}) collective-permute-start(bf16[224,4096]{1,0:T(8,128)(2,1)} %get-tuple-element.398), channel_id=1, source_target_pairs={{4,8},{8,4},{5,9},{9,5},{6,10},{10,6},{7,11},{11,7},{20,24},{24,20... | collective-permute-start | bytes 5505032 | tf_op jit(solution)/shard_map/cond/branch_5_fun/ppermute | solution.py:541
  32.0 1.2 %copy-start = (bf16[224,4096]{1,0:T(8,128)(2,1)}, bf16[224,4096]{1,0:T(8,128)(2,1)S(1)}, u32[]{:S(2)}) copy-start(bf16[224,4096]{1,0:T(8,128)(2,1)S(1)} %collective-permute-done.76.refs_0_) | copy-start | bytes 5505028 | tf_op jit(solution)/shard_map/cond
  33.2 29.6 %collective-permute-start.78 = (bf16[224,4096]{1,0:T(8,128)(2,1)}, bf16[224,4096]{1,0:T(8,128)(2,1)S(1)}, u32[]{:S(2)}, u32[]{:S(2)}) collective-permute-start(bf16[224,4096]{1,0:T(8,128)(2,1)} %copy-done), channel_id=1, source_target_pairs={{4,5},{8,9},{5,4},{9,8},{6,7},{10,11},{7,6},{11,10},{20,21},{24,25... | collective-permute-start | bytes 5505032 | tf_op jit(solution)/shard_map/cond/branch_5_fun/ppermute | solution.py:541
  36.4 26.4 %collective-permute-start.77 = (bf16[224,4096]{1,0:T(8,128)(2,1)}, bf16[224,4096]{1,0:T(8,128)(2,1)}, u32[]{:S(2)}, u32[]{:S(2)}) collective-permute-start(bf16[224,4096]{1,0:T(8,128)(2,1)} %copy-done), channel_id=1, source_target_pairs={{4,20},{8,24},{5,21},{9,25},{6,22},{10,26},{7,23},{11,27},{20,4},{... | collective-permute-start | bytes 5505032 | tf_op jit(solution)/shard_map/cond/branch_5_fun/ppermute | solution.py:541
  39.9 4.0 %collective-permute-start.79 = (f32[32,2048]{1,0:T(8,128)S(1)}, f32[32,2048]{1,0:T(8,128)S(1)}, u32[]{:S(2)}, u32[]{:S(2)}) collective-permute-start(f32[32,2048]{1,0:T(8,128)S(1)} %constant_dynamic-slice_fusion.17), channel_id=1, source_target_pairs={{0,4},{4,0},{8,12},{12,8},{1,5},{5,1},{9,13},{13,9},{2,6},{6,2},{1... | collective-permute-start | bytes 786440 | tf_op jit(solution)/shard_map/cond/branch_5_fun/ppermute | solution.py:541
  43.9 23.9 %copy-start.36 = (bf16[320,4096]{1,0:T(8,128)(2,1)S(1)}, bf16[320,4096]{1,0:T(8,128)(2,1)}, u32[]{:S(2)}) copy-start(bf16[320,4096]{1,0:T(8,128)(2,1)} %get-tuple-element.412) | copy-start | bytes 7864324 | tf_op jit(solution)/shard_map/cond
  43.9 31.1 %copy-start.1 = (bf16[224,4096]{1,0:T(8,128)(2,1)S(1)}, bf16[224,4096]{1,0:T(8,128)(2,1)}, u32[]{:S(2)}) copy-start(bf16[224,4096]{1,0:T(8,128)(2,1)} %copy-done) | copy-start | bytes 5505028 | tf_op jit(solution)/shard_map/cond
  44.0 10.9 %collective-permute-start.80 = (bf16[32,2048]{1,0:T(8,128)(2,1)S(1)}, bf16[32,2048]{1,0:T(8,128)(2,1)S(1)}, u32[]{:S(2)}, u32[]{:S(2)}) collective-permute-start(bf16[32,2048]{1,0:T(8,128)(2,1)S(1)} %add_convert_fusion.11), channel_id=1, source_target_pairs={{0,8},{4,12},{8,0},{12,4},{1,9},{5,13},{9,1},{13,5},{2,10},{6,14},... | collective-permute-start | bytes 393224 | tf_op jit(solution)/shard_map/cond/branch_5_fun/ppermute | solution.py:541
  46.7 16.2 %collective-permute-start.81 = (bf16[160,1792]{1,0:T(8,128)(2,1)S(1)}, bf16[160,1792]{1,0:T(8,128)(2,1)S(1)}, u32[]{:S(2)}, u32[]{:S(2)}) collective-permute-start(bf16[160,1792]{1,0:T(8,128)(2,1)S(1)} %constant_dynamic-slice_fusion.16), channel_id=1, source_target_pairs={{4,8},{8,4},{5,9},{9,5},{6,10},{10,6},{7,11},{11,7},{20,24},{24,20... | collective-permute-start | bytes 1720328 | tf_op jit(solution)/shard_map/cond/branch_5_fun/ppermute | solution.py:541
  54.9 5.6 %collective-permute-start.82 = (bf16[160,896]{1,0:T(8,128)(2,1)S(1)}, bf16[160,896]{1,0:T(8,128)(2,1)S(1)}, u32[]{:S(2)}, u32[]{:S(2)}) collective-permute-start(bf16[160,896]{1,0:T(8,128)(2,1)S(1)} %constant_dynamic-slice_fusion.15), channel_id=1, source_target_pairs={{4,0},{8,12},{5,1},{9,13},{6,2},{10,14},{7,3},{11,15},{20,16},{24,... | collective-permute-start | bytes 860168 | tf_op jit(solution)/shard_map/cond/branch_5_fun/ppermute | solution.py:541
  62.8 32.0 %collective-permute-start.88 = (bf16[896,4096]{1,0:T(8,128)(2,1)}, bf16[896,4096]{1,0:T(8,128)(2,1)S(1)}, u32[]{:S(2)}, u32[]{:S(2)}) collective-permute-start(bf16[896,4096]{1,0:T(8,128)(2,1)} %get-tuple-element.414), channel_id=1, source_target_pairs={{4,0},{8,12},{5,1},{9,13},{6,2},{10,14},{7,3},{11,15},{20,16},{24,... | collective-permute-start | bytes 22020104 | tf_op jit(solution)/shard_map/cond/branch_5_fun/ppermute | solution.py:541
  64.6 24.2 %collective-permute-start.87 = (bf16[224,4096]{1,0:T(8,128)(2,1)}, bf16[224,4096]{1,0:T(8,128)(2,1)S(1)}, u32[]{:S(2)}, u32[]{:S(2)}) collective-permute-start(bf16[224,4096]{1,0:T(8,128)(2,1)} %collective-permute-done.75.refs_1_), channel_id=1, source_target_pairs={{4,5},{8,9},{5,4},{9,8},{6,7},{10,11},{7,6},{11,10},{20,21},{24,25... | collective-permute-start | bytes 5505032 | tf_op jit(solution)/shard_map/cond/branch_5_fun/ppermute | solution.py:541
  67.8 33.0 %collective-permute-start.85 = (bf16[320,4096]{1,0:T(8,128)(2,1)S(1)}, bf16[320,4096]{1,0:T(8,128)(2,1)S(1)}, u32[]{:S(2)}, u32[]{:S(2)}) collective-permute-start(bf16[320,4096]{1,0:T(8,128)(2,1)S(1)} %copy-done.36), channel_id=1, source_target_pairs={{4,8},{8,4},{5,9},{9,5},{6,10},{10,6},{7,11},{11,7},{20,24},{24,20... | collective-permute-start | bytes 7864328 | tf_op jit(solution)/shard_map/cond/branch_5_fun/ppermute | solution.py:541
  70.7 24.2 %collective-permute-start.86 = (bf16[224,4096]{1,0:T(8,128)(2,1)}, bf16[224,4096]{1,0:T(8,128)(2,1)S(1)}, u32[]{:S(2)}, u32[]{:S(2)}) collective-permute-start(bf16[224,4096]{1,0:T(8,128)(2,1)} %collective-permute-done.75.refs_1_), channel_id=1, source_target_pairs={{4,20},{8,24},{5,21},{9,25},{6,22},{10,26},{7,23},{11,27},{20,4},{... | collective-permute-start | bytes 5505032 | tf_op jit(solution)/shard_map/cond/branch_5_fun/ppermute | solution.py:541
  73.8 12.1 %collective-permute-start.89 = (bf16[32,2048]{1,0:T(8,128)(2,1)S(1)}, bf16[32,2048]{1,0:T(8,128)(2,1)S(1)}, u32[]{:S(2)}, u32[]{:S(2)}) collective-permute-start(bf16[32,2048]{1,0:T(8,128)(2,1)S(1)} %add_convert_fusion.10), channel_id=1, source_target_pairs={{0,4},{4,0},{8,12},{12,8},{1,5},{5,1},{9,13},{13,9},{2,6},{6,2},{1... | collective-permute-start | bytes 393224 | tf_op jit(solution)/shard_map/cond/branch_5_fun/ppermute | solution.py:541
  85.9 9.9 %collective-permute-start.84 = (bf16[64,4096]{1,0:T(8,128)(2,1)S(1)}, bf16[64,4096]{1,0:T(8,128)(2,1)S(1)}, u32[]{:S(2)}, u32[]{:S(2)}) collective-permute-start(bf16[64,4096]{1,0:T(8,128)(2,1)S(1)} %slice.53), channel_id=1, source_target_pairs={{4,5},{8,9},{5,4},{9,8},{6,7},{10,11},{7,6},{11,10},{20,21},{24,25... | collective-permute-start | bytes 1572872 | tf_op jit(solution)/shard_map/cond/branch_5_fun/ppermute | solution.py:541
  88.8 11.7 %collective-permute-start.83 = (bf16[64,4096]{1,0:T(8,128)(2,1)S(1)}, bf16[64,4096]{1,0:T(8,128)(2,1)S(1)}, u32[]{:S(2)}, u32[]{:S(2)}) collective-permute-start(bf16[64,4096]{1,0:T(8,128)(2,1)S(1)} %slice.52), channel_id=1, source_target_pairs={{4,20},{8,24},{5,21},{9,25},{6,22},{10,26},{7,23},{11,27},{20,4},{... | collective-permute-start | bytes 1572872 | tf_op jit(solution)/shard_map/cond/branch_5_fun/ppermute | solution.py:541

commit v2 on v1

--- a/solution.py
+++ b/solution.py
@@ -468,7 +468,7 @@
 
 
 def split(blocks):
-    return blocks, (3 * blocks + 5) // 11
+    return blocks, (2 * blocks + 5) // 11
 
 
 def neighbours(x, z, dt, enter, leave, w, ssm, conv, logs, taps, offs, inc, res, ranks, tallies):

time: 102 us -> 104 us (1.020); the launches traced: 102 us -> 102 us
  transfers between devices with their start and end apart: 15 -> 15, of which waited for: 8 -> 7; matrix products, arithmetic and copies ran while one was open for 3% -> 3% of each run, Pallas kernels for 29% -> 29%
where the time goes in v2:
time: 104 us; the launch traced here: 102 us
  starting transfers between devices  38.8 us (37%)
  Pallas kernels  35.1 us (34%)
  waiting for transfers between devices  18 us (17%)
  loops' own time  4.7 us (5%)
  local copies, waits for them, and re-layouts  3.2 us (3%)
  between operations  1.51 us (1%)
    ppermute x15, starting transfers between devices, permute(): return lax.ppermute(a, AXES, pairs)  38.8 us
    ppermute x15, waiting for transfers between devices, permute(): return lax.ppermute(a, AXES, pairs)  18 us
    pallas_call x1, Pallas kernels, decode_here(): pl.pallas_call(decode_kernel, grid_spec=grid_spec, out_shape=(jax.ShapeDt...  17.8 us
    pallas_call x3, Pallas kernels, place_rows(): pl.pallas_call(kernel, grid_spec=pltpu.PrefetchScalarGridSpec(num_scalar_...  10.7 us
    another operation x1, loops' own time, neighbours(): decoded, out_w, new_ssm, new_conv = lax.switch(pick, branches, args)  4.7 us
    pallas_call x1, Pallas kernels, cut_rows(): pl.pallas_call(kernel, grid_spec=pltpu.PrefetchScalarGridSpec(num_scalar_...  3.28 us
  transfers between devices with their start and end apart: 15, of which 7 were waited for; matrix products, arithmetic and copies ran while one was open for 3% of the time, Pallas kernels for 29%

profile of v2, /device:TPU:1, one launch (start us, length us, event | category | flops | bytes accessed | tf_op | source)
XLA Modules:
  0.0 102.1 jit_solution(7223331858284573228)
XLA Ops:
  0.6 1.3 %plan.1 = (s32[1]{0:T(128)}, s32[15]{0:T(128)S(1)}, s32[1]{0:T(128)}, s32[1]{0:T(128)}) custom-call(s32[3]{0:T(128)} %ranks.1, s32[3]{0:T(128)} %tallies.1), custom_call_target="tpu_custom_call" | custom-call | tf_op jit(solution)/shard_map/plan/pallas_call | solution.py:531
  2.6 99.3 %conditional.1 = (bf16[2944,4096]{1,0:T(8,128)(2,1)}, f32[2944,128]{1,0:T(8,128)}, f32[32,2944]{1,0:T(8,128)}, bf16[4,8,4096]{2,1,0:T(8,128)(2,1)}) conditional(s32[]{:T(128)} %bitcast.72, (s32[15]{0:T(128)S(1)}, bf16[2048,4096]{1,0:T(8,128)(2,1)}, f32[4,8,16]{2,1,0:T(8,128)}, f32[4,8,16]{2,1,0:T(8,128)}, ...), branch_computations={%region_0.1_spmd, %region_1.2_spmd, %region_2.3_spmd, %region_3.4_... | conditional | flops 1048592 | bytes 118959080 | solution.py:620
  2.9 3.3 %cut_rows.11 = bf16[224,4096]{1,0:T(8,128)(2,1)} custom-call(s32[15]{0:T(128)S(1)} %get-tuple-element.411.sc, bf16[2048,4096]{1,0:T(8,128)(2,1)} %get-tuple-element.384.w_ref.w_all), custom_call_target="tpu_custom_call" | custom-call | bytes 1024 | tf_op jit(solution)/shard_map/cond/branch_5_fun/cut_rows/pallas_call | solution.py:287
  6.2 4.7 %collective-permute-start.76 = (bf16[224,4096]{1,0:T(8,128)(2,1)}, bf16[224,4096]{1,0:T(8,128)(2,1)S(1)}, u32[]{:S(2)}, u32[]{:S(2)}) collective-permute-start(bf16[224,4096]{1,0:T(8,128)(2,1)} %cut_rows.11), channel_id=1, source_target_pairs={{4,8},{8,4},{5,9},{9,5},{6,10},{10,6},{7,11},{11,7},{20,24},{24,20... | collective-permute-start | bytes 5505032 | tf_op jit(solution)/shard_map/cond/branch_5_fun/ppermute | solution.py:541
  11.4 17.8 %decode.11 = (bf16[2944,4096]{1,0:T(8,128)(2,1)}, bf16[896,4096]{1,0:T(8,128)(2,1)}, bf16[224,4096]{1,0:T(8,128)(2,1)}, bf16[352,4096]{1,0:T(8,128)(2,1)}, f32[3...) custom-call(s32[15]{0:T(128)S(1)} %get-tuple-element.411.sc, bf16[4,8,2048]{2,1,0:T(8,128)(2,1)} %get-tuple-element.386.x, ...), custom_call_target="tpu_custom_call" | custom-call | bytes 1024 | tf_op jit(solution)/shard_map/cond/branch_5_fun/decode/pallas_call | solution.py:253
  29.3 2.5 %collective-permute-start.75 = (bf16[224,4096]{1,0:T(8,128)(2,1)}, bf16[224,4096]{1,0:T(8,128)(2,1)}, u32[]{:S(2)}, u32[]{:S(2)}) collective-permute-start(bf16[224,4096]{1,0:T(8,128)(2,1)} %get-tuple-element.398), channel_id=1, source_target_pairs={{4,8},{8,4},{5,9},{9,5},{6,10},{10,6},{7,11},{11,7},{20,24},{24,20... | collective-permute-start | bytes 5505032 | tf_op jit(solution)/shard_map/cond/branch_5_fun/ppermute | solution.py:541
  32.0 1.2 %copy-done = bf16[224,4096]{1,0:T(8,128)(2,1)} copy-done((bf16[224,4096]{1,0:T(8,128)(2,1)}, bf16[224,4096]{1,0:T(8,128)(2,1)S(1)}, u32[]{:S(2)}) %copy-start) | copy-done | bytes 1835032 | tf_op jit(solution)/shard_map/cond
  33.2 3.2 %collective-permute-start.78 = (bf16[224,4096]{1,0:T(8,128)(2,1)}, bf16[224,4096]{1,0:T(8,128)(2,1)S(1)}, u32[]{:S(2)}, u32[]{:S(2)}) collective-permute-start(bf16[224,4096]{1,0:T(8,128)(2,1)} %copy-done), channel_id=1, source_target_pairs={{4,5},{8,9},{5,4},{9,8},{6,7},{10,11},{7,6},{11,10},{20,21},{24,25... | collective-permute-start | bytes 5505032 | tf_op jit(solution)/shard_map/cond/branch_5_fun/ppermute | solution.py:541
  36.4 3.1 %collective-permute-start.77 = (bf16[224,4096]{1,0:T(8,128)(2,1)}, bf16[224,4096]{1,0:T(8,128)(2,1)}, u32[]{:S(2)}, u32[]{:S(2)}) collective-permute-start(bf16[224,4096]{1,0:T(8,128)(2,1)} %copy-done), channel_id=1, source_target_pairs={{4,20},{8,24},{5,21},{9,25},{6,22},{10,26},{7,23},{11,27},{20,4},{... | collective-permute-start | bytes 5505032 | tf_op jit(solution)/shard_map/cond/branch_5_fun/ppermute | solution.py:541
  43.5 2.5 %collective-permute-start.80 = (bf16[32,2048]{1,0:T(8,128)(2,1)S(1)}, bf16[32,2048]{1,0:T(8,128)(2,1)S(1)}, u32[]{:S(2)}, u32[]{:S(2)}) collective-permute-start(bf16[32,2048]{1,0:T(8,128)(2,1)S(1)} %add_convert_fusion.11), channel_id=1, source_target_pairs={{0,8},{4,12},{8,0},{12,4},{1,9},{5,13},{9,1},{13,5},{2,10},{6,14},... | collective-permute-start | bytes 393224 | tf_op jit(solution)/shard_map/cond/branch_5_fun/ppermute | solution.py:541
  46.2 2.2 %collective-permute-start.81 = (bf16[160,1792]{1,0:T(8,128)(2,1)S(1)}, bf16[160,1792]{1,0:T(8,128)(2,1)S(1)}, u32[]{:S(2)}, u32[]{:S(2)}) collective-permute-start(bf16[160,1792]{1,0:T(8,128)(2,1)S(1)} %constant_dynamic-slice_fusion.16), channel_id=1, source_target_pairs={{4,8},{8,4},{5,9},{9,5},{6,10},{10,6},{7,11},{11,7},{20,24},{24,20... | collective-permute-start | bytes 1720328 | tf_op jit(solution)/shard_map/cond/branch_5_fun/ppermute | solution.py:541
  48.6 6.4 %collective-permute-done.80 = bf16[32,2048]{1,0:T(8,128)(2,1)S(1)} collective-permute-done((bf16[32,2048]{1,0:T(8,128)(2,1)S(1)}, bf16[32,2048]{1,0:T(8,128)(2,1)S(1)}, u32[]{:S(2)}, u32[]{:S(2)}) %collective-permute-start.80) | collective-permute-done | bytes 131104 | tf_op jit(solution)/shard_map/cond/branch_5_fun/ppermute | solution.py:541
  55.0 4.5 %collective-permute-start.82 = (bf16[160,896]{1,0:T(8,128)(2,1)S(1)}, bf16[160,896]{1,0:T(8,128)(2,1)S(1)}, u32[]{:S(2)}, u32[]{:S(2)}) collective-permute-start(bf16[160,896]{1,0:T(8,128)(2,1)S(1)} %constant_dynamic-slice_fusion.15), channel_id=1, source_target_pairs={{4,0},{8,12},{5,1},{9,13},{6,2},{10,14},{7,3},{11,15},{20,16},{24,... | collective-permute-start | bytes 860168 | tf_op jit(solution)/shard_map/cond/branch_5_fun/ppermute | solution.py:541
  60.6 2.4 %collective-permute-done.81.across_ref = bf16[160,1792]{1,0:T(8,128)(2,1)S(1)} collective-permute-done((bf16[160,1792]{1,0:T(8,128)(2,1)S(1)}, bf16[160,1792]{1,0:T(8,128)(2,1)S(1)}, u32[]{:S(2)}, u32[]{:S(2)}) %collective-permute-start.81) | collective-permute-done | bytes 573472 | tf_op jit(solution)/shard_map/cond/branch_5_fun/ppermute | solution.py:541
  63.0 1.8 %collective-permute-start.88 = (bf16[896,4096]{1,0:T(8,128)(2,1)}, bf16[896,4096]{1,0:T(8,128)(2,1)S(1)}, u32[]{:S(2)}, u32[]{:S(2)}) collective-permute-start(bf16[896,4096]{1,0:T(8,128)(2,1)} %get-tuple-element.414), channel_id=1, source_target_pairs={{4,0},{8,12},{5,1},{9,13},{6,2},{10,14},{7,3},{11,15},{20,16},{24,... | collective-permute-start | bytes 22020104 | tf_op jit(solution)/shard_map/cond/branch_5_fun/ppermute | solution.py:541
  64.8 2.8 %collective-permute-start.85 = (bf16[352,4096]{1,0:T(8,128)(2,1)}, bf16[352,4096]{1,0:T(8,128)(2,1)S(1)}, u32[]{:S(2)}, u32[]{:S(2)}) collective-permute-start(bf16[352,4096]{1,0:T(8,128)(2,1)} %get-tuple-element.412), channel_id=1, source_target_pairs={{4,8},{8,4},{5,9},{9,5},{6,10},{10,6},{7,11},{11,7},{20,24},{24,20... | collective-permute-start | bytes 8650760 | tf_op jit(solution)/shard_map/cond/branch_5_fun/ppermute | solution.py:541
  67.6 2.9 %collective-permute-start.87 = (bf16[224,4096]{1,0:T(8,128)(2,1)}, bf16[224,4096]{1,0:T(8,128)(2,1)S(1)}, u32[]{:S(2)}, u32[]{:S(2)}) collective-permute-start(bf16[224,4096]{1,0:T(8,128)(2,1)} %collective-permute-done.75.refs_1_), channel_id=1, source_target_pairs={{4,5},{8,9},{5,4},{9,8},{6,7},{10,11},{7,6},{11,10},{20,21},{24,25... | collective-permute-start | bytes 5505032 | tf_op jit(solution)/shard_map/cond/branch_5_fun/ppermute | solution.py:541
  70.5 3.1 %collective-permute-start.86 = (bf16[224,4096]{1,0:T(8,128)(2,1)}, bf16[224,4096]{1,0:T(8,128)(2,1)S(1)}, u32[]{:S(2)}, u32[]{:S(2)}) collective-permute-start(bf16[224,4096]{1,0:T(8,128)(2,1)} %collective-permute-done.75.refs_1_), channel_id=1, source_target_pairs={{4,20},{8,24},{5,21},{9,25},{6,22},{10,26},{7,23},{11,27},{20,4},{... | collective-permute-start | bytes 5505032 | tf_op jit(solution)/shard_map/cond/branch_5_fun/ppermute | solution.py:541
  74.8 8.9 %place_rows.33.refs_3_ = bf16[2944,4096]{1,0:T(8,128)(2,1)} custom-call(s32[15]{0:T(128)S(1)} %get-tuple-element.411.sc, bf16[224,4096]{1,0:T(8,128)(2,1)S(1)} %copy-done.1, bf16[224,4096]{1,0:T(8,128)(2,1)} %collective-permute-done.75.refs_1_, bf16[224,4096]{1,0:T(8,128)(2,1)} %collective-permute-done.77.refs_2_, ...), custom_call_target="tpu_custom_call", output_to_operand_aliasing={{}: (5, {})} | custom-call | bytes 1024 | tf_op jit(solution)/shard_map/cond/branch_5_fun/place_rows/pallas_call | solution.py:391
  83.7 1.9 %place_states.11 = (f32[2944,128]{1,0:T(8,128)}, f32[32,2944]{1,0:T(8,128)}) custom-call(s32[15]{0:T(128)S(1)} %get-tuple-element.411.sc, bf16[160,2048]{1,0:T(8,128)(2,1)S(1)} %get-tuple-element.406.own_ref, bf16[160,896]{1,0:T(8,128)(2,1)S(1)} %collective-permute-done.82.side_ref, bf16[160,1792]{1,0:T(8,128)(2,1)S(1)} %collective-permute-done.81.across_ref), custom_call_target="tpu_custom_call" | custom-call | bytes 1024 | tf_op jit(solution)/shard_map/cond/branch_5_fun/place_states/pallas_call | solution.py:451
  85.7 2.3 %collective-permute-start.84 = (bf16[48,4096]{1,0:T(8,128)(2,1)S(1)}, bf16[48,4096]{1,0:T(8,128)(2,1)S(1)}, u32[]{:S(2)}, u32[]{:S(2)}) collective-permute-start(bf16[48,4096]{1,0:T(8,128)(2,1)S(1)} %slice.53), channel_id=1, source_target_pairs={{4,5},{8,9},{5,4},{9,8},{6,7},{10,11},{7,6},{11,10},{20,21},{24,25... | collective-permute-start | bytes 1179656 | tf_op jit(solution)/shard_map/cond/branch_5_fun/ppermute | solution.py:541
  88.1 3.7 %collective-permute-done.87.refs_1_ = bf16[224,4096]{1,0:T(8,128)(2,1)S(1)} collective-permute-done((bf16[224,4096]{1,0:T(8,128)(2,1)}, bf16[224,4096]{1,0:T(8,128)(2,1)S(1)}, u32[]{:S(2)}, u32[]{:S(2)}) %collective-permute-start.87) | collective-permute-done | bytes 1835040 | tf_op jit(solution)/shard_map/cond/branch_5_fun/ppermute | solution.py:541
  91.7 3.1 %collective-permute-start.83 = (bf16[48,4096]{1,0:T(8,128)(2,1)S(1)}, bf16[48,4096]{1,0:T(8,128)(2,1)S(1)}, u32[]{:S(2)}, u32[]{:S(2)}) collective-permute-start(bf16[48,4096]{1,0:T(8,128)(2,1)S(1)} %slice.52), channel_id=1, source_target_pairs={{4,20},{8,24},{5,21},{9,25},{6,22},{10,26},{7,23},{11,27},{20,4},{... | collective-permute-start | bytes 1179656 | tf_op jit(solution)/shard_map/cond/branch_5_fun/ppermute | solution.py:541
  96.5 3.7 %collective-permute-done.83.refs_0_ = bf16[48,4096]{1,0:T(8,128)(2,1)S(1)} collective-permute-done((bf16[48,4096]{1,0:T(8,128)(2,1)S(1)}, bf16[48,4096]{1,0:T(8,128)(2,1)S(1)}, u32[]{:S(2)}, u32[]{:S(2)}) %collective-permute-start.83) | collective-permute-done | bytes 393248 | tf_op jit(solution)/shard_map/cond/branch_5_fun/ppermute | solution.py:541
  (39 shorter events, 6.5 us)
Async XLA Ops:
  2.9 8.0 %copy-start.19 = (f32[2048,32]{0,1:T(8,128)S(1)}, f32[2048,32]{0,1:T(8,128)}, u32[]{:S(2)}) copy-start(f32[2048,32]{0,1:T(8,128)} %get-tuple-element.392) | copy-start | bytes 786436 | tf_op jit(solution)/shard_map/cond
  2.9 8.3 %copy-start.29 = (f32[4,8,16]{2,1,0:T(8,128)S(1)}, f32[4,8,16]{2,1,0:T(8,128)}, u32[]{:S(2)}) copy-start(f32[4,8,16]{2,1,0:T(8,128)} %get-tuple-element.389) | copy-start | bytes 6148 | tf_op jit(solution)/shard_map/cond
  2.9 8.4 %copy-start.35 = (f32[4,8,16]{2,1,0:T(8,128)S(1)}, f32[4,8,16]{2,1,0:T(8,128)}, u32[]{:S(2)}) copy-start(f32[4,8,16]{2,1,0:T(8,128)} %get-tuple-element.390) | copy-start | bytes 6148 | tf_op jit(solution)/shard_map/cond
  6.2 5.2 %copy-start.13 = (f32[8192,16]{0,1:T(8,128)S(1)}, f32[8192,16]{0,1:T(8,128)}, u32[]{:S(2)}) copy-start(f32[8192,16]{0,1:T(8,128)} %get-tuple-element.393) | copy-start | bytes 1572868 | tf_op jit(solution)/shard_map/cond
  6.2 25.8 %collective-permute-start.76 = (bf16[224,4096]{1,0:T(8,128)(2,1)}, bf16[224,4096]{1,0:T(8,128)(2,1)S(1)}, u32[]{:S(2)}, u32[]{:S(2)}) collective-permute-start(bf16[224,4096]{1,0:T(8,128)(2,1)} %cut_rows.11), channel_id=1, source_target_pairs={{4,8},{8,4},{5,9},{9,5},{6,10},{10,6},{7,11},{11,7},{20,24},{24,20... | collective-permute-start | bytes 5505032 | tf_op jit(solution)/shard_map/cond/branch_5_fun/ppermute | solution.py:541
  29.3 30.2 %collective-permute-start.75 = (bf16[224,4096]{1,0:T(8,128)(2,1)}, bf16[224,4096]{1,0:T(8,128)(2,1)}, u32[]{:S(2)}, u32[]{:S(2)}) collective-permute-start(bf16[224,4096]{1,0:T(8,128)(2,1)} %get-tuple-element.398), channel_id=1, source_target_pairs={{4,8},{8,4},{5,9},{9,5},{6,10},{10,6},{7,11},{11,7},{20,24},{24,20... | collective-permute-start | bytes 5505032 | tf_op jit(solution)/shard_map/cond/branch_5_fun/ppermute | solution.py:541
  32.0 1.2 %copy-start = (bf16[224,4096]{1,0:T(8,128)(2,1)}, bf16[224,4096]{1,0:T(8,128)(2,1)S(1)}, u32[]{:S(2)}) copy-start(bf16[224,4096]{1,0:T(8,128)(2,1)S(1)} %collective-permute-done.76.refs_0_) | copy-start | bytes 5505028 | tf_op jit(solution)/shard_map/cond
  33.2 29.8 %collective-permute-start.78 = (bf16[224,4096]{1,0:T(8,128)(2,1)}, bf16[224,4096]{1,0:T(8,128)(2,1)S(1)}, u32[]{:S(2)}, u32[]{:S(2)}) collective-permute-start(bf16[224,4096]{1,0:T(8,128)(2,1)} %copy-done), channel_id=1, source_target_pairs={{4,5},{8,9},{5,4},{9,8},{6,7},{10,11},{7,6},{11,10},{20,21},{24,25... | collective-permute-start | bytes 5505032 | tf_op jit(solution)/shard_map/cond/branch_5_fun/ppermute | solution.py:541
  36.4 26.6 %collective-permute-start.77 = (bf16[224,4096]{1,0:T(8,128)(2,1)}, bf16[224,4096]{1,0:T(8,128)(2,1)}, u32[]{:S(2)}, u32[]{:S(2)}) collective-permute-start(bf16[224,4096]{1,0:T(8,128)(2,1)} %copy-done), channel_id=1, source_target_pairs={{4,20},{8,24},{5,21},{9,25},{6,22},{10,26},{7,23},{11,27},{20,4},{... | collective-permute-start | bytes 5505032 | tf_op jit(solution)/shard_map/cond/branch_5_fun/ppermute | solution.py:541
  39.6 3.8 %collective-permute-start.79 = (f32[32,2048]{1,0:T(8,128)S(1)}, f32[32,2048]{1,0:T(8,128)S(1)}, u32[]{:S(2)}, u32[]{:S(2)}) collective-permute-start(f32[32,2048]{1,0:T(8,128)S(1)} %constant_dynamic-slice_fusion.17), channel_id=1, source_target_pairs={{0,4},{4,0},{8,12},{12,8},{1,5},{5,1},{9,13},{13,9},{2,6},{6,2},{1... | collective-permute-start | bytes 786440 | tf_op jit(solution)/shard_map/cond/branch_5_fun/ppermute | solution.py:541
  43.5 31.3 %copy-start.1 = (bf16[224,4096]{1,0:T(8,128)(2,1)S(1)}, bf16[224,4096]{1,0:T(8,128)(2,1)}, u32[]{:S(2)}) copy-start(bf16[224,4096]{1,0:T(8,128)(2,1)} %copy-done) | copy-start | bytes 5505028 | tf_op jit(solution)/shard_map/cond
  43.5 11.5 %collective-permute-start.80 = (bf16[32,2048]{1,0:T(8,128)(2,1)S(1)}, bf16[32,2048]{1,0:T(8,128)(2,1)S(1)}, u32[]{:S(2)}, u32[]{:S(2)}) collective-permute-start(bf16[32,2048]{1,0:T(8,128)(2,1)S(1)} %add_convert_fusion.11), channel_id=1, source_target_pairs={{0,8},{4,12},{8,0},{12,4},{1,9},{5,13},{9,1},{13,5},{2,10},{6,14},... | collective-permute-start | bytes 393224 | tf_op jit(solution)/shard_map/cond/branch_5_fun/ppermute | solution.py:541
  46.2 16.8 %collective-permute-start.81 = (bf16[160,1792]{1,0:T(8,128)(2,1)S(1)}, bf16[160,1792]{1,0:T(8,128)(2,1)S(1)}, u32[]{:S(2)}, u32[]{:S(2)}) collective-permute-start(bf16[160,1792]{1,0:T(8,128)(2,1)S(1)} %constant_dynamic-slice_fusion.16), channel_id=1, source_target_pairs={{4,8},{8,4},{5,9},{9,5},{6,10},{10,6},{7,11},{11,7},{20,24},{24,20... | collective-permute-start | bytes 1720328 | tf_op jit(solution)/shard_map/cond/branch_5_fun/ppermute | solution.py:541
  55.0 5.6 %collective-permute-start.82 = (bf16[160,896]{1,0:T(8,128)(2,1)S(1)}, bf16[160,896]{1,0:T(8,128)(2,1)S(1)}, u32[]{:S(2)}, u32[]{:S(2)}) collective-permute-start(bf16[160,896]{1,0:T(8,128)(2,1)S(1)} %constant_dynamic-slice_fusion.15), channel_id=1, source_target_pairs={{4,0},{8,12},{5,1},{9,13},{6,2},{10,14},{7,3},{11,15},{20,16},{24,... | collective-permute-start | bytes 860168 | tf_op jit(solution)/shard_map/cond/branch_5_fun/ppermute | solution.py:541
  63.0 32.6 %collective-permute-start.88 = (bf16[896,4096]{1,0:T(8,128)(2,1)}, bf16[896,4096]{1,0:T(8,128)(2,1)S(1)}, u32[]{:S(2)}, u32[]{:S(2)}) collective-permute-start(bf16[896,4096]{1,0:T(8,128)(2,1)} %get-tuple-element.414), channel_id=1, source_target_pairs={{4,0},{8,12},{5,1},{9,13},{6,2},{10,14},{7,3},{11,15},{20,16},{24,... | collective-permute-start | bytes 22020104 | tf_op jit(solution)/shard_map/cond/branch_5_fun/ppermute | solution.py:541
  64.8 36.0 %collective-permute-start.85 = (bf16[352,4096]{1,0:T(8,128)(2,1)}, bf16[352,4096]{1,0:T(8,128)(2,1)S(1)}, u32[]{:S(2)}, u32[]{:S(2)}) collective-permute-start(bf16[352,4096]{1,0:T(8,128)(2,1)} %get-tuple-element.412), channel_id=1, source_target_pairs={{4,8},{8,4},{5,9},{9,5},{6,10},{10,6},{7,11},{11,7},{20,24},{24,20... | collective-permute-start | bytes 8650760 | tf_op jit(solution)/shard_map/cond/branch_5_fun/ppermute | solution.py:541
  67.6 24.2 %collective-permute-start.87 = (bf16[224,4096]{1,0:T(8,128)(2,1)}, bf16[224,4096]{1,0:T(8,128)(2,1)S(1)}, u32[]{:S(2)}, u32[]{:S(2)}) collective-permute-start(bf16[224,4096]{1,0:T(8,128)(2,1)} %collective-permute-done.75.refs_1_), channel_id=1, source_target_pairs={{4,5},{8,9},{5,4},{9,8},{6,7},{10,11},{7,6},{11,10},{20,21},{24,25... | collective-permute-start | bytes 5505032 | tf_op jit(solution)/shard_map/cond/branch_5_fun/ppermute | solution.py:541
  70.5 25.1 %collective-permute-start.86 = (bf16[224,4096]{1,0:T(8,128)(2,1)}, bf16[224,4096]{1,0:T(8,128)(2,1)S(1)}, u32[]{:S(2)}, u32[]{:S(2)}) collective-permute-start(bf16[224,4096]{1,0:T(8,128)(2,1)} %collective-permute-done.75.refs_1_), channel_id=1, source_target_pairs={{4,20},{8,24},{5,21},{9,25},{6,22},{10,26},{7,23},{11,27},{20,4},{... | collective-permute-start | bytes 5505032 | tf_op jit(solution)/shard_map/cond/branch_5_fun/ppermute | solution.py:541
  73.6 12.0 %collective-permute-start.89 = (bf16[32,2048]{1,0:T(8,128)(2,1)S(1)}, bf16[32,2048]{1,0:T(8,128)(2,1)S(1)}, u32[]{:S(2)}, u32[]{:S(2)}) collective-permute-start(bf16[32,2048]{1,0:T(8,128)(2,1)S(1)} %add_convert_fusion.10), channel_id=1, source_target_pairs={{0,4},{4,0},{8,12},{12,8},{1,5},{5,1},{9,13},{13,9},{2,6},{6,2},{1... | collective-permute-start | bytes 393224 | tf_op jit(solution)/shard_map/cond/branch_5_fun/ppermute | solution.py:541
  85.7 10.8 %collective-permute-start.84 = (bf16[48,4096]{1,0:T(8,128)(2,1)S(1)}, bf16[48,4096]{1,0:T(8,128)(2,1)S(1)}, u32[]{:S(2)}, u32[]{:S(2)}) collective-permute-start(bf16[48,4096]{1,0:T(8,128)(2,1)S(1)} %slice.53), channel_id=1, source_target_pairs={{4,5},{8,9},{5,4},{9,8},{6,7},{10,11},{7,6},{11,10},{20,21},{24,25... | collective-permute-start | bytes 1179656 | tf_op jit(solution)/shard_map/cond/branch_5_fun/ppermute | solution.py:541
  91.7 8.5 %collective-permute-start.83 = (bf16[48,4096]{1,0:T(8,128)(2,1)S(1)}, bf16[48,4096]{1,0:T(8,128)(2,1)S(1)}, u32[]{:S(2)}, u32[]{:S(2)}) collective-permute-start(bf16[48,4096]{1,0:T(8,128)(2,1)S(1)} %slice.52), channel_id=1, source_target_pairs={{4,20},{8,24},{5,21},{9,25},{6,22},{10,26},{7,23},{11,27},{20,4},{... | collective-permute-start | bytes 1179656 | tf_op jit(solution)/shard_map/cond/branch_5_fun/ppermute | solution.py:541
